TPU v7x, 512 devices: a whole 4x4x16 slice. The times are simulated.
512 devices in a mesh: depth: 8 (over z_hi, core), lat: 64 (over x, z_lo, y).
Axes of the slice: x: 4, y: 4, z: 16 (z_hi: 4, z_lo: 4; z = z_hi * 4 + z_lo), core: 2. Of those that a mesh axis runs over, the one named last changes fastest.
Arguments:
- fields: float32 [6, 384, 64, 512], P(None, 'lat', 'depth'), may hold values from -3 to 3
- material: int32 [384, 64, 512], P('lat', 'depth'), may hold values from 0 to 3
- source_mask: int32 [384, 64, 512], P('lat', 'depth'), may hold values 0 or 1
- eps_table: float32 [4], replicated, may hold values from 1 to 6
- kerr_table: float32 [4], replicated, may hold values from 0.3 to 3
Outputs:
- fields_out: float32 [6, 384, 64, 512], P(None, 'lat', 'depth')
- image: float32 [384, 8, 512], P('lat', None, 'depth')
Inputs may be any that keep to these rules, and one draw needn't show every extreme that they name: material indexes the tables.
All inputs are finite; a program needn't handle non-finite values. No bound on the sum of `source_mask` on one device may be relied on, other than what follows from the above.
Results may differ from a plain program's by a relative error of at most 0.0003.
Values sent between devices are 32-bit elements; how exact they have to be, the bound alone decides.
A program may use at most 64 MiB of HBM per device.

v0:
```python
import math

import jax
import jax.numpy as jnp
from jax import lax
from jax.sharding import PartitionSpec as P

STEPS = 16


COURANT = 0.55
OMEGAS = (0.9, 1.3)
SOURCE_AMP = 1.0
QUARTERS = (3, 5)
HIGHEST = lax.Precision.HIGHEST


def padded_2(block, sides, width):
    for axis, dim in sides:
        count = lax.axis_size(axis)
        forward = [(i, i + 1) for i in range(count - 1)]
        backward = [(target, source) for source, target in forward]
        low = lax.ppermute(
            lax.slice_in_dim(block, block.shape[dim] - width, None, axis=dim), axis, forward
        )
        high = lax.ppermute(lax.slice_in_dim(block, 0, width, axis=dim), axis, backward)
        block = jnp.concatenate([low, block, high], axis=dim)
    return block


def from_root(block, axis, owner):
    block = jnp.where(lax.axis_index(axis) == owner, block, jnp.zeros_like(block))
    return lax.psum(block, axis)


def forward_diff(field, along):
    length = field.shape[along]
    ahead = lax.slice_in_dim(field, 1, length, axis=along)
    ahead = jnp.concatenate(
        [ahead, jnp.zeros_like(lax.slice_in_dim(field, 0, 1, axis=along))], axis=along
    )
    return ahead - field


def backward_diff(field, along):
    length = field.shape[along]
    behind = lax.slice_in_dim(field, 0, length - 1, axis=along)
    behind = jnp.concatenate(
        [jnp.zeros_like(lax.slice_in_dim(field, 0, 1, axis=along)), behind], axis=along
    )
    return field - behind


def drive(moment):
    middle = moment + 0.5
    return SOURCE_AMP * (jnp.sin(OMEGAS[0] * middle) + jnp.sin(OMEGAS[1] * middle))


def yee_step(fields, permittivity, kerr_coef, source_flag, inside, pulse):
    elec_x, elec_y, elec_z = (fields[0], fields[1], fields[2])
    magn_x, magn_y, magn_z = (fields[3], fields[4], fields[5])
    magn_x = (magn_x - COURANT * (forward_diff(elec_z, 2) - forward_diff(elec_y, 1))) * inside
    magn_y = (magn_y - COURANT * (forward_diff(elec_x, 1) - forward_diff(elec_z, 0))) * inside
    magn_z = (magn_z - COURANT * (forward_diff(elec_y, 0) - forward_diff(elec_x, 2))) * inside
    energy = elec_x * elec_x + elec_y * elec_y + elec_z * elec_z
    factor = COURANT / (permittivity + kerr_coef * energy)
    new_x = (
        elec_x
        + factor * (backward_diff(magn_z, 2) - backward_diff(magn_y, 1))
        + source_flag * pulse
    ) * inside
    new_y = (elec_y + factor * (backward_diff(magn_x, 1) - backward_diff(magn_z, 0))) * inside
    new_z = (elec_z + factor * (backward_diff(magn_y, 0) - backward_diff(magn_x, 2))) * inside
    return jnp.stack([new_x, new_y, new_z, magn_x, magn_y, magn_z])


def lookup(material, table):
    result = jnp.zeros(material.shape, jnp.float32)
    for level in range(table.shape[0]):
        result = jnp.where(material == level, table[level], result)
    return result


def accumulate(spectrum, plane, moment):
    later = moment + 1.0
    trig = jnp.stack(
        [jnp.stack([jnp.cos(omega * later), -jnp.sin(omega * later)]) for omega in OMEGAS]
    )
    return spectrum + trig[:, None, :, None, None] * plane[None, :, None, :, :]


def chirp(row_index, col_index, length):
    gap = row_index[:, None] - col_index[None, :]
    squared = gap * gap
    reals, imags = ([], [])
    for quarter in QUARTERS:
        wrapped = quarter * squared % (8 * length)
        phase = wrapped.astype(jnp.float32) * (math.pi / (4.0 * length))
        reals.append(jnp.cos(phase) / math.sqrt(length))
        imags.append(jnp.sin(phase) / math.sqrt(length))
    return (jnp.stack(reals), jnp.stack(imags))


def column_transform(real, imag, y_real, y_imag):
    v_real = jnp.einsum("fcxy,fyk->fcxk", real, y_real, precision=HIGHEST) - jnp.einsum(
        "fcxy,fyk->fcxk", imag, y_imag, precision=HIGHEST
    )
    v_imag = jnp.einsum("fcxy,fyk->fcxk", real, y_imag, precision=HIGHEST) + jnp.einsum(
        "fcxy,fyk->fcxk", imag, y_real, precision=HIGHEST
    )
    return (v_real, v_imag)


def row_transform(x_real, x_imag, v_real, v_imag):
    w_real = jnp.einsum("fix,fcxk->ifck", x_real, v_real, precision=HIGHEST) - jnp.einsum(
        "fix,fcxk->ifck", x_imag, v_imag, precision=HIGHEST
    )
    w_imag = jnp.einsum("fix,fcxk->ifck", x_real, v_imag, precision=HIGHEST) + jnp.einsum(
        "fix,fcxk->ifck", x_imag, v_real, precision=HIGHEST
    )
    return jnp.stack([w_real, w_imag], axis=3)


def local(fields, material, source_mask, eps_table, kerr_table):
    width_x = fields.shape[1]
    depth_z = fields.shape[2]
    span_y = fields.shape[3]
    lat_count = lax.axis_size("lat")
    depth_count = lax.axis_size("depth")
    total_x = width_x * lat_count
    total_z = depth_z * depth_count
    lat_pos = lax.axis_index("lat")
    depth_pos = lax.axis_index("depth")
    coefs = jnp.stack(
        [lookup(material, eps_table), lookup(material, kerr_table), source_mask.astype(jnp.float32)]
    )
    empty_spectrum = jnp.zeros((2, 2, 2, width_x, span_y), jnp.float32)
    rim_width = ((0, 0), (1, 1), (1, 1), (0, 0))
    eps_pad = jnp.pad(coefs[0:1], rim_width, constant_values=1.0)
    rest_pad = jnp.pad(coefs[1:3], rim_width, constant_values=0.0)
    sub = jnp.concatenate([eps_pad, rest_pad], axis=0)
    place_x = lat_pos * width_x - 1 + jnp.arange(width_x + 2 * 1, dtype=jnp.int32)
    place_z = depth_pos * depth_z - 1 + jnp.arange(depth_z + 2 * 1, dtype=jnp.int32)
    valid_x = (place_x >= 0) & (place_x < total_x)
    valid_z = (place_z >= 0) & (place_z < total_z)
    valid = valid_x[:, None] & valid_z[None, :]
    setup_inside = valid.astype(jnp.float32)[:, :, None]
    setup_permittivity = jnp.where(valid[:, :, None], sub[0], 1.0)
    kerr_coef = sub[1]
    source_flag = sub[2]

    def one_step(step, carry):
        state, spectrum = carry
        padded = padded_2(state, (("depth", 2), ("lat", 1)), 1)
        moment = step.astype(jnp.float32)
        padded = yee_step(
            padded, setup_permittivity, kerr_coef, source_flag, setup_inside, drive(moment)
        )
        state = padded[:, 1:-1, 1:-1]
        spectrum = accumulate(spectrum, state[0:2, :, depth_z - 1, :], moment)
        return (state, spectrum)

    state, spectrum = lax.fori_loop(0, STEPS, one_step, (fields, empty_spectrum))
    spectrum = from_root(spectrum, "depth", depth_count - 1)
    col_count = span_y // depth_count
    col_index = depth_pos * col_count + jnp.arange(col_count, dtype=jnp.int32)
    y_real, y_imag = chirp(jnp.arange(span_y, dtype=jnp.int32), col_index, span_y)
    v_real, v_imag = column_transform(spectrum[:, :, 0], spectrum[:, :, 1], y_real, y_imag)
    row_local = lat_pos * width_x + jnp.arange(width_x, dtype=jnp.int32)
    row_index = jnp.arange(width_x * lax.axis_size("lat"), dtype=jnp.int32)
    x_real, x_imag = chirp(row_index, row_local, total_x)
    image = lax.psum_scatter(
        row_transform(x_real, x_imag, v_real, v_imag), "lat", scatter_dimension=0, tiled=True
    )
    return (state, image.reshape(width_x, 8, col_count))


def solution(mesh):
    placed = (
        P(None, "lat", "depth", None),
        P("lat", "depth", None),
        P("lat", "depth", None),
        P(),
        P(),
    )
    return jax.shard_map(
        local,
        mesh=mesh,
        in_specs=placed,
        out_specs=(P(None, "lat", "depth", None), P("lat", None, "depth")),
        check_vma=False,
    )
```

profile of v0, /device:TPU:8, one launch (start us, length us, event | category | flops | bytes accessed | tf_op | source)
XLA Modules:
  0.0 1378.4 jit_solution(10861475274174279404)
XLA Ops:
  11.0 5.2 select_bitcast_fusion
  17.2 478.5 %while.16 = (s32[]{:T(128)}, f32[6,6,8,512]{3,0,1,2:T(8,128)S(1)}, f32[2,2,2,6,512]{4,3,2,1,0:T(8,128)S(1)}, f32[8,10,512]{2,0,1:T(8,128)S(1)}, f32[8,10,512]{2,...) while((s32[]{:T(128)}, f32[6,6,8,512]{3,0,1,2:T(8,128)S(1)}, ...), condition=%wide.region_1.2_spmd.clone, body=%wide.region_0.1_spmd.clone.sunk | while | flops 2527413 | bytes 23437268 | solution.py:163
  21.4 8.1 collective-permute-done.1
  29.7 2.4 collective-permute-start.2
  32.1 3.5 collective-permute-start.3
  36.5 2.4 collective-permute-done.3
  45.5 7.6 collective-permute-start
  55.2 2.2 collective-permute-done.1
  57.6 1.9 collective-permute-start.2
  59.5 3.9 collective-permute-start.3
  64.4 1.9 collective-permute-done.3
  72.9 12.7 collective-permute-start
  89.2 1.9 collective-permute-start.2
  91.2 4.3 collective-permute-start.3
  104.6 8.2 collective-permute-start
  116.4 1.9 collective-permute-start.2
  118.4 7.1 collective-permute-start.3
  134.5 8.2 collective-permute-start
  146.4 1.9 collective-permute-start.2
  148.3 6.9 collective-permute-start.3
  164.3 8.0 collective-permute-start
  176.0 1.9 collective-permute-start.2
  177.9 5.9 collective-permute-start.3
  192.8 8.9 collective-permute-start
  205.4 1.9 collective-permute-start.2
  207.4 6.7 collective-permute-start.3
  223.1 8.6 collective-permute-start
  235.4 1.9 collective-permute-start.2
  237.3 6.1 collective-permute-start.3
  252.5 9.4 collective-permute-start
  267.4 7.0 collective-permute-start.3
  283.5 10.1 collective-permute-start
  299.4 6.7 collective-permute-start.3
  315.1 10.7 collective-permute-start
  331.4 5.8 collective-permute-start.3
  346.2 8.2 collective-permute-start
  360.0 6.3 collective-permute-start.3
  375.4 8.7 collective-permute-start
  389.7 6.8 collective-permute-start.3
  405.5 8.9 collective-permute-start
  420.1 7.4 collective-permute-start.3
  436.5 8.6 collective-permute-start
  450.7 6.9 collective-permute-start.3
  466.7 10.0 collective-permute-start
  482.3 4.7 collective-permute-start.3
  497.7 143.1 %all-reduce.18.cloned.1.call-done = f32[2,2,2,6,512]{4,3,1,0,2:T(8,128)} async-done(((f32[2,2,2,6,512]{4,3,1,0,2:T(8,128)}), f32[2,2,2,6,512]{4,3,1,0,2:T(8,128)}) %all-reduce.18.cloned.1.call-update) | async-done | bytes 98320 | tf_op jit(solution)/shard_map/psum | solution.py:33
  648.2 2.1 copy.46
  653.4 716.9 %all-reduce.20.cloned.1.call-done = f32[384,2,2,2,64]{4,3,2,1,0:T(2,128)} async-done(((f32[384,2,2,2,64]{4,3,2,1,0:T(2,128)}), f32[384,2,2,2,64]{4,3,2,1,0:T(2,128)}) %all-reduce.20.cloned.1.call-update) | async-done | bytes 786448
  (667 shorter events, 221.3 us)
Async XLA Ops:
  7.2 633.7 %all-reduce.18.cloned.1.call-start = ((), (), s32[]{:S(2)}) async-start(), calls=%async_computation | async-start | bytes 262144 | tf_op jit(solution)/shard_map/psum | solution.py:33
  19.3 10.2 collective-permute-start.1
  29.7 6.8 collective-permute-start.2
  32.1 6.8 collective-permute-start.3
  45.5 9.3 collective-permute-start
  72.9 14.4 %collective-permute-start = (f32[6,6,1,512]{3,1,2,0:T(8,128)S(1)}, f32[6,6,1,512]{3,1,2,0:T(8,128)S(1)}, u32[]{:S(2)}, u32[]{:S(2)}) collective-permute-start(f32[6,6,1,512]{3,1,2,0:T(8,128)S(1)} %get-tuple-element.301), channel_id=1, source_target_pairs={{0,64},{64,128},{128,192},{192,256},{256,320},{320,384},{384,448},... | collective-permute-start | bytes 221192 | tf_op jit(solution)/shard_map/while/body/eval_jaxpr/ppermute | solution.py:23
  89.2 7.2 collective-permute-start.2
  91.2 6.8 collective-permute-start.3
  104.6 9.9 collective-permute-start
  116.4 10.0 collective-permute-start.2
  118.4 9.6 collective-permute-start.3
  134.5 9.9 collective-permute-start
  146.4 9.8 collective-permute-start.2
  148.3 9.3 collective-permute-start.3
  164.3 9.7 collective-permute-start
  176.0 8.8 collective-permute-start.2
  177.9 8.3 collective-permute-start.3
  192.8 10.6 collective-permute-start
  205.4 9.6 collective-permute-start.2
  207.4 9.2 collective-permute-start.3
  223.1 10.3 collective-permute-start
  235.4 8.9 collective-permute-start.2
  237.3 8.5 collective-permute-start.3
  252.5 11.1 collective-permute-start
  265.5 9.9 collective-permute-start.2
  267.4 9.5 collective-permute-start.3
  283.5 11.8 collective-permute-start
  297.5 9.5 collective-permute-start.2
  299.4 9.1 collective-permute-start.3
  315.1 12.4 collective-permute-start
  329.5 8.6 collective-permute-start.2
  331.4 8.2 collective-permute-start.3
  346.2 9.9 collective-permute-start
  358.1 9.2 collective-permute-start.2
  360.0 8.8 collective-permute-start.3
  375.4 10.4 collective-permute-start
  387.8 9.6 collective-permute-start.2
  389.7 9.2 collective-permute-start.3
  405.5 10.6 collective-permute-start
  418.1 10.3 collective-permute-start.2
  420.1 9.9 collective-permute-start.3
  436.5 10.3 collective-permute-start
  448.8 9.8 collective-permute-start.2
  450.7 9.4 collective-permute-start.3
  466.7 11.7 collective-permute-start
  480.3 7.6 collective-permute-start.2
  482.3 7.2 collective-permute-start.3
  496.4 873.9 %all-reduce.20.cloned.1.call-start = ((), (), s32[]{:S(2)}) async-start(), calls=%async_computation.1 | async-start | bytes 3145728
  (37 other events, 91.4 us)
Sparse Core Ops, SparseCore 0:
  496.5 144.3 all-reduce.17
  650.4 719.8 all-reduce.19
where the time goes:
time: 1380 us
  waiting for transfers between devices  924 us (67%)
  starting transfers between devices  287 us (21%)
  local copies, waits for them, and re-layouts  81.5 us (6%)
  other arithmetic  52.3 us (4%)
  between operations  14.9 us (1%)
    unnamed x3, waiting for transfers between devices  717 us
    ppermute x32, starting transfers between devices, padded_2(): lax.ppermute(lax.slice_in_dim(block, block.shape[dim] - width, None, axis...  235 us
    psum x1, waiting for transfers between devices, from_root(): return lax.psum(block, axis)  143 us
    ppermute x32, starting transfers between devices, padded_2(): lax.ppermute(lax.slice_in_dim(block, 0, width, axis=dim), axis, backward)  51.8 us
    another operation x112, local copies, waits for them, and re-layouts, yee_step(): return jnp.stack([new_x, new_y, new_z, magn_x, magn_y, magn_z])  40.2 us
    ppermute x32, waiting for transfers between devices, padded_2(): lax.ppermute(lax.slice_in_dim(block, 0, width, axis=dim), axis, backward)  38.8 us
  transfers between devices with their start and end apart: 66, of which 50 were waited for; matrix products, arithmetic and copies ran while one was open for 1% of the time, Pallas kernels for 0%

commit v1 on v0

v1 whole, which is shorter than its diff:
```python
import functools
import math

import jax
import jax.numpy as jnp
import numpy as np
from jax import lax
from jax.experimental import pallas as pl
from jax.experimental.pallas import tpu as pltpu
from jax.sharding import PartitionSpec as P

STEPS = 16
COURANT = 0.55
OMEGAS = (0.9, 1.3)
QUARTERS = (3, 5)
HIGHEST = lax.Precision.HIGHEST
MESH = pl.DeviceIdType.MESH


def pulses():
    middle = np.arange(STEPS) + 0.5
    return np.asarray(np.sin(OMEGAS[0] * middle) + np.sin(OMEGAS[1] * middle), np.float32)


def turns():
    later = np.arange(STEPS) + 1.0
    parts = []
    for omega in OMEGAS:
        parts += [np.cos(omega * later), -np.sin(omega * later)]
    return np.asarray(np.stack(parts, axis=1), np.float32)


def chirp(length):
    gap = np.arange(length)[:, None] - np.arange(length)[None, :]
    reals, imags = [], []
    for quarter in QUARTERS:
        phase = (quarter * gap * gap % (8 * length)) * (math.pi / (4.0 * length))
        reals.append(np.cos(phase) / math.sqrt(length))
        imags.append(np.sin(phase) / math.sqrt(length))
    return np.asarray(np.stack(reals), np.float32), np.asarray(np.stack(imags), np.float32)


def step_kernel(
    count_z, count_x,
    fields_ref, material_ref, mask_ref, eps_ref, kerr_ref, pulse_ref, turn_ref,
    state, spec,
    eps_v, kerr_v, src_v, fac_v,
    rows_e, rows_h, rows_top, corner_s,
    in_xe, in_xh, in_ze, in_zh, in_c,
    send_sem, recv_sem,
):
    wide = state.shape[1]
    span = state.shape[3]
    last = wide - 1
    pos_z = lax.axis_index("depth")
    pos_x = lax.axis_index("lat")
    has_lx, has_hx = pos_x > 0, pos_x < count_x - 1
    has_lz, has_hz = pos_z > 0, pos_z < count_z - 1
    has_a = has_lz & has_hx
    has_b = has_hz & has_lx
    to_lx, to_hx = (pos_z, pos_x - 1), (pos_z, pos_x + 1)
    to_lz, to_hz = (pos_z - 1, pos_x), (pos_z + 1, pos_x)
    to_a, to_b = (pos_z - 1, pos_x + 1), (pos_z + 1, pos_x - 1)
    neighbours = (
        (has_lx, to_lx), (has_hx, to_hx), (has_lz, to_lz), (has_hz, to_hz), (has_a, to_a), (has_b, to_b)
    )

    in_xe[...] = jnp.zeros_like(in_xe)
    in_xh[...] = jnp.zeros_like(in_xh)
    in_ze[...] = jnp.zeros_like(in_ze)
    in_zh[...] = jnp.zeros_like(in_zh)
    in_c[...] = jnp.zeros_like(in_c)

    barrier = pltpu.get_barrier_semaphore()
    for has, target in neighbours:
        @pl.when(has)
        def _():
            pl.semaphore_signal(barrier, inc=1, device_id=target, device_id_type=MESH)

    material = material_ref[...]
    eps, kerr = jnp.zeros(material.shape, jnp.float32), jnp.zeros(material.shape, jnp.float32)
    for level in range(eps_ref.shape[0]):
        eps = jnp.where(material == level, eps_ref[level], eps)
        kerr = jnp.where(material == level, kerr_ref[level], kerr)
    eps_v[...] = eps
    kerr_v[...] = kerr
    src_v[...] = mask_ref[...].astype(jnp.float32)
    state[...] = fields_ref[...]
    spec[...] = jnp.zeros_like(spec)

    pl.semaphore_wait(barrier, sum(jnp.where(has, 1, 0) for has, _ in neighbours))

    row = lax.broadcasted_iota(jnp.int32, (8, span), 0)
    col = lax.broadcasted_iota(jnp.int32, (8, span), 1)
    top_row, first_row = row == 7, row == 0
    top_col, first_col = col == span - 1, col == 0
    s = jnp.float32(COURANT)
    keep_lx = jnp.where(has_lx, 1.0, 0.0).astype(jnp.float32)
    keep_lz = jnp.where(has_lz, 1.0, 0.0).astype(jnp.float32)

    def next_y(f):
        return jnp.where(top_col, 0.0, pltpu.roll(f, span - 1, 1))

    def prev_y(f):
        return jnp.where(first_col, 0.0, pltpu.roll(f, 1, 1))

    def next_z(f):
        return jnp.where(top_row, 0.0, pltpu.roll(f, 7, 0))

    def wide_row(r):
        return jnp.broadcast_to(r, (8, span))

    def one_step(n, carry):
        slot = lax.rem(n, 2)

        def copy(index, source, target, there, sem):
            return pltpu.make_async_remote_copy(
                src_ref=source, dst_ref=there, send_sem=send_sem.at[index],
                recv_sem=recv_sem.at[slot, sem], device_id=target, device_id_type=MESH,
            )

        for x in range(wide):
            rows_e[0, x : x + 1, :] = state[0, x, 0:1, :]
            rows_e[1, x : x + 1, :] = state[1, x, 0:1, :]
        corner_s[0:1, :] = state[2, 0, 7:8, :]
        out_lx = copy(0, state.at[1:3, 0], to_lx, in_xe.at[slot], 0)
        out_lz = copy(1, rows_e, to_lz, in_ze.at[slot], 1)
        out_a = copy(2, rows_e.at[0, last : last + 1], to_a, in_c.at[slot, 0], 2)
        out_b = copy(3, corner_s, to_b, in_c.at[slot, 1], 3)
        for has, item in ((has_a, out_a), (has_b, out_b), (has_lx, out_lx), (has_lz, out_lz)):
            @pl.when(has)
            def _():
                item.start()

        for x in [last] + list(range(last)):
            ex, ey, ez = state[0, x], state[1, x], state[2, x]
            if x < last:
                ahead_y, ahead_z = state[1, x + 1], state[2, x + 1]
            else:
                ahead_y, ahead_z = jnp.zeros_like(ey), jnp.zeros_like(ez)
            hx = state[3, x] - s * ((next_y(ez) - ez) - (next_z(ey) - ey))
            hy = state[4, x] - s * ((next_z(ex) - ex) - (ahead_z - ez))
            hz = state[5, x] - s * ((ahead_y - ey) - (next_y(ex) - ex))
            state[3, x] = hx
            state[4, x] = hy
            state[5, x] = hz
            rows_h[0, x : x + 1, :] = hx[7:8, :]
            rows_h[1, x : x + 1, :] = hy[7:8, :]
        out_hx = copy(4, state.at[4:6, last], to_hx, in_xh.at[slot], 4)
        out_hz = copy(5, rows_h, to_hz, in_zh.at[slot], 5)
        for has, item in ((has_hz, out_hz), (has_hx, out_hx)):
            @pl.when(has)
            def _():
                item.start()

        for x in range(wide):
            ex, ey, ez = state[0, x], state[1, x], state[2, x]
            fac_v[x] = s / (eps_v[x] + kerr_v[x] * (ex * ex + ey * ey + ez * ez))

        for has, sem, there in (
            (has_hx, 0, in_xe), (has_lx, 4, in_xh), (has_hz, 1, in_ze), (has_lz, 5, in_zh),
        ):
            @pl.when(has)
            def _():
                pltpu.make_async_remote_copy(
                    src_ref=there.at[slot], dst_ref=there.at[slot], send_sem=send_sem.at[sem],
                    recv_sem=recv_sem.at[slot, sem], device_id=to_lx, device_id_type=MESH,
                ).wait_recv()
        for has, sem, place in ((has_b, 2, 0), (has_a, 3, 1)):
            @pl.when(has)
            def _():
                pltpu.make_async_remote_copy(
                    src_ref=in_c.at[slot, place], dst_ref=in_c.at[slot, place], send_sem=send_sem.at[sem],
                    recv_sem=recv_sem.at[slot, sem], device_id=to_lx, device_id_type=MESH,
                ).wait_recv()
        for has, item in (
            (has_lx, out_lx), (has_lz, out_lz), (has_a, out_a), (has_b, out_b), (has_hx, out_hx), (has_hz, out_hz)
        ):
            @pl.when(has)
            def _():
                item.wait_send()

        ex, ey, ez = state[0, 0], state[1, 0], state[2, 0]
        corner_x = jnp.where(top_row, wide_row(in_c[slot, 0]), 0.0)
        before_y = keep_lx * (in_xh[slot, 0] + s * ez - s * corner_x)
        before_z = keep_lx * (in_xh[slot, 1] - s * ey)
        pulse = pulse_ref[n]
        for x in range(wide):
            ex, ey, ez = state[0, x], state[1, x], state[2, x]
            above_x = wide_row(in_ze[slot, 0, x : x + 1, :])
            above_y = wide_row(in_ze[slot, 1, x : x + 1, :])
            hx = state[3, x] + jnp.where(top_row, s * above_y, 0.0)
            hy = state[4, x] - jnp.where(top_row, s * above_x, 0.0)
            hz = state[5, x]
            below_x = wide_row(in_zh[slot, 0, x : x + 1, :]) + s * ey
            below_y = wide_row(in_zh[slot, 1, x : x + 1, :]) - s * ex
            if x == last:
                hy = hy + s * in_xe[slot, 1]
                hz = hz - s * in_xe[slot, 0]
                below_y = below_y + s * wide_row(in_c[slot, 1])
            down_x = jnp.where(first_row, keep_lz * below_x, pltpu.roll(hx, 1, 0))
            down_y = jnp.where(first_row, keep_lz * below_y, pltpu.roll(hy, 1, 0))
            fac = fac_v[x]
            state[0, x] = ex + fac * ((hz - prev_y(hz)) - (hy - down_y)) + src_v[x] * pulse
            state[1, x] = ey + fac * ((hx - down_x) - (hz - before_z))
            state[2, x] = ez + fac * ((hy - before_y) - (hx - prev_y(hx)))
            state[3, x] = hx
            state[4, x] = hy
            state[5, x] = hz
            before_y, before_z = hy, hz

        @pl.when(pos_z == count_z - 1)
        def _():
            for x in range(wide):
                rows_top[0, x : x + 1, :] = state[0, x, 7:8, :]
                rows_top[1, x : x + 1, :] = state[1, x, 7:8, :]
            for f in range(2):
                for part in range(2):
                    weight = turn_ref[n, 2 * f + part]
                    for c in range(2):
                        spec[4 * f + 2 * c + part] += weight * rows_top[c]

        return carry

    lax.fori_loop(0, STEPS, one_step, 0)


def march(count_z, count_x, fields, material, mask, eps_table, kerr_table):
    _, wide, deep, span = fields.shape
    vmem = pl.BlockSpec(memory_space=pltpu.VMEM)
    smem = pl.BlockSpec(memory_space=pltpu.SMEM)
    f32 = jnp.float32
    return pl.pallas_call(
        functools.partial(step_kernel, count_z, count_x),
        out_shape=(
            jax.ShapeDtypeStruct(fields.shape, f32),
            jax.ShapeDtypeStruct((8, wide, span), f32),
        ),
        in_specs=[vmem, vmem, vmem, smem, smem, smem, smem],
        out_specs=(vmem, vmem),
        scratch_shapes=[
            pltpu.VMEM((wide, deep, span), f32),
            pltpu.VMEM((wide, deep, span), f32),
            pltpu.VMEM((wide, deep, span), f32),
            pltpu.VMEM((wide, deep, span), f32),
            pltpu.VMEM((2, wide, span), f32),
            pltpu.VMEM((2, wide, span), f32),
            pltpu.VMEM((2, wide, span), f32),
            pltpu.VMEM((1, span), f32),
            pltpu.VMEM((2, 2, deep, span), f32),
            pltpu.VMEM((2, 2, deep, span), f32),
            pltpu.VMEM((2, 2, wide, span), f32),
            pltpu.VMEM((2, 2, wide, span), f32),
            pltpu.VMEM((2, 2, 1, span), f32),
            pltpu.SemaphoreType.DMA((6,)),
            pltpu.SemaphoreType.DMA((2, 6)),
        ],
        compiler_params=pltpu.CompilerParams(
            collective_id=1, has_side_effects=True, vmem_limit_bytes=32 * 1024 * 1024
        ),
        name="march",
    )(fields, material, mask, eps_table, kerr_table, jnp.asarray(pulses()), jnp.asarray(turns()))


def local(fields, material, source_mask, eps_table, kerr_table):
    _, wide, deep, span = fields.shape
    count_x, count_z = lax.axis_size("lat"), lax.axis_size("depth")
    state, spec = march(count_z, count_x, fields, material, source_mask, eps_table, kerr_table)
    spec = spec.reshape(2, 2, 2, wide, span)
    y_real, y_imag = (jnp.asarray(part) for part in chirp(span))
    both = jnp.concatenate([y_real, y_imag], axis=2)
    prod = jnp.einsum("fcpxy,fyk->fcpxk", spec, both, precision=HIGHEST)
    v_real = prod[:, :, 0, :, :span] - prod[:, :, 1, :, span:]
    v_imag = prod[:, :, 0, :, span:] + prod[:, :, 1, :, :span]
    v = jnp.stack([v_real, v_imag])
    cols = span // count_z
    v = v.reshape(8 * wide, count_z, cols).transpose(1, 0, 2)
    v = lax.all_to_all(v, "depth", 0, 0)[count_z - 1]
    per = cols // count_x
    v = v.reshape(2, 2, 2, wide, count_x, per).transpose(4, 0, 1, 2, 3, 5)
    v = lax.all_to_all(v, "lat", 0, 0)
    v = v.transpose(2, 0, 4, 1, 3, 5).reshape(2, count_x * wide, 2 * 2 * per)
    x_real, x_imag = (jnp.asarray(part) for part in chirp(count_x * wide))
    both = jnp.concatenate([x_real, x_imag], axis=1)
    w = jnp.einsum("fix,fxn->fin", both, v, precision=HIGHEST)
    total = count_x * wide
    w = w.reshape(2, 2, total, 2, 2, per)
    w_real = w[:, 0, :, 0] - w[:, 1, :, 1]
    w_imag = w[:, 0, :, 1] + w[:, 1, :, 0]
    w = jnp.stack([w_real, w_imag], axis=3)
    w = w.transpose(1, 0, 2, 3, 4).reshape(count_x, wide, 8, per)
    w = lax.all_to_all(w, "lat", 0, 0)
    image = w.transpose(1, 2, 0, 3).reshape(wide, 8, cols)
    return state, image


def solution(mesh):
    placed = (P(None, "lat", "depth", None), P("lat", "depth", None), P("lat", "depth", None), P(), P())
    return jax.shard_map(
        local, mesh=mesh, in_specs=placed,
        out_specs=(P(None, "lat", "depth", None), P("lat", None, "depth")), check_vma=False,
    )
```

time: 1380 us -> 203 us (0.15)
  the two profiles are of different devices: /device:TPU:8 before, /device:TPU:1 now
where the time goes in v1:
time: 203 us; the launch traced here: 202 us
  Pallas kernels  94.3 us (46%)
  blocking collectives  73.2 us (36%)
  waiting for transfers between devices  10 us (5%)
  local copies, waits for them, and re-layouts  9.8 us (5%)
  matrix products  6.77 us (3%)
  starting transfers between devices  6.52 us (3%)
    pallas_call x1, Pallas kernels, march(): pl.pallas_call(functools.partial(step_kernel, count_z, count_x), out_shap...  94.3 us
    all_to_all x1, blocking collectives, local(): v = lax.all_to_all(v, 'lat', 0, 0)  51.9 us
    all_to_all x1, blocking collectives, local(): v = lax.all_to_all(v, 'depth', 0, 0)[count_z - 1]  21.3 us
    all_to_all x1, waiting for transfers between devices, local(): w = lax.all_to_all(w, 'lat', 0, 0)  10 us
    unnamed x19, local copies, waits for them, and re-layouts  6.57 us
    all_to_all x1, starting transfers between devices, local(): w = lax.all_to_all(w, 'lat', 0, 0)  6.52 us
    dot_general x1, matrix products, local(): prod = jnp.einsum('fcpxy,fyk->fcpxk', spec, both, precision=HIGHEST)  4.7 us
  transfers between devices with their start and end apart: 1, of which 1 were waited for; matrix products, arithmetic and copies ran while one was open for 0% of the time, Pallas kernels for 0%

profile of v1, /device:TPU:1, one launch (start us, length us, event | category | flops | bytes accessed | tf_op | source)
XLA Modules:
  0.0 202.3 jit_solution(16508418636914124277)
XLA Ops:
  0.6 0.0 copy-start
  0.6 1.1 copy-done
  1.7 0.0 copy-start.1
  1.7 0.9 copy-done.1
  2.6 0.0 copy-start.2
  2.6 0.9 copy-done.2
  3.5 0.0 copy-start.3
  3.5 0.7 copy-done.3
  4.2 0.0 copy-start.4
  4.2 0.7 copy-done.4
  4.8 0.0 copy-start.5
  4.8 0.7 copy-done.5
  5.5 0.0 copy-start.6
  5.5 0.7 copy-done.6
  6.1 94.3 %march.1 = (f32[6,6,8,512]{3,2,1,0:T(8,128)S(1)}, f32[8,6,512]{2,1,0:T(8,128)S(1)}) custom-call(f32[6,6,8,512]{3,2,1,0:T(8,128)S(1)} %copy-done, s32[6,8,512]{2,1,0:T(8,128)S(1)} %copy-done.1, s32[6,8,512]{2,1,0:T(8,128)S(1)} %copy-done.2, f32[4]{0:T(128)S(1)} %copy-done.4, f32[4]{0:T(128)S(1)} %copy-done.5, f32[16]{0:T(128)S(1)} %copy-done.6, ...), custom_call_target="tpu_custom_call" | custom-call | tf_op jit(solution)/shard_map/march/pallas_call | solution.py:233
  100.4 0.0 copy-start.7
  100.5 4.7 %fusion.7 = f32[2,2,2,6,1024]{4,3,2,1,0:T(8,128)S(1)} fusion(f32[2,2,2,6,512]{4,3,2,1,0:T(8,128)S(1)} %bitcast.64, f32[2,512,1024,1,1]{2,1,4,3,0:T(8,128)} %constant.23), kind=kOutput, calls=%fused_computation.16 | convolution fusion | flops 301989888 | bytes 4489216 | tf_op jit(solution)/shard_map/fcpxy,fyk->fcpxk/dot_general | solution.py:272
  105.2 0.1 reshape.105
  105.4 0.2 reshape.111
  105.5 21.3 %all_to_all.15 = f32[8,1,3072]{2,1,0:T(1,128)S(1)} all-to-all(f32[8,1,3072]{2,1,0:T(1,128)S(1)} %reshape.111), channel_id=1, replica_groups=mesh['depth'=8,'lat'=64] {'depth'}, dimensions={0} | all-to-all | bytes 196608 | tf_op jit(solution)/shard_map/all_to_all | solution.py:278
  126.8 0.5 broadcast
  127.3 0.9 reduce
  128.2 0.1 reshape.112
  128.3 0.2 copy.40
  128.6 51.9 %all_to_all.16 = f32[64,2,2,2,6,1]{4,3,1,2,5,0:T(2,128)S(1)} all-to-all(f32[64,2,2,2,6,1]{4,3,1,2,5,0:T(2,128)S(1)} %copy.40), channel_id=1, replica_groups=mesh['depth'=8,'lat'=64] {'lat'}, dimensions={0} | all-to-all | bytes 24576 | tf_op jit(solution)/shard_map/all_to_all | solution.py:281
  180.5 0.1 copy.41
  180.5 0.2 reshape.106
  180.7 0.0 copy-done.7
  180.7 2.1 %fusion.8 = f32[2,768,4]{1,2,0:T(4,128)S(1)} fusion(f32[2,768,384]{2,1,0:T(8,128)S(1)} %copy-done.7, f32[2,384,4]{1,2,0:T(4,128)S(1)} %reshape.106), kind=kOutput, calls=%fused_computation.17 | convolution fusion | flops 28311552 | bytes 2396160 | tf_op jit(solution)/shard_map/fix,fxn->fin/dot_general | solution.py:285
  182.9 0.2 reshape.108
  183.1 1.1 copy.46
  184.3 6.5 %all-to-all-start.2 = ((f32[64,6,8,1]{2,3,1,0:T(1,128)}), f32[64,6,8,1]{2,3,1,0:T(1,128)S(1)}, u32[]{:S(2)}, u32[]{:S(2)}) async-start(f32[64,6,8,1]{2,3,1,0:T(1,128)} %copy.46), calls=%async_computation.2 | async-start | bytes 393216 | tf_op jit(solution)/shard_map/all_to_all | solution.py:292
  190.8 10.0 %all-to-all-done.2 = f32[64,6,8,1]{2,3,1,0:T(1,128)S(1)} async-done(((f32[64,6,8,1]{2,3,1,0:T(1,128)}), f32[64,6,8,1]{2,3,1,0:T(1,128)S(1)}, u32[]{:S(2)}, u32[]{:S(2)}) %all-to-all-start.2) | async-done | bytes 12320 | tf_op jit(solution)/shard_map/all_to_all | solution.py:292
  200.8 0.7 copy.47
  201.5 0.8 copy.56
  (8 shorter events, 0.2 us)
Async XLA Ops:
  0.6 1.1 copy-start
  1.7 0.9 copy-start.1
  2.6 0.9 copy-start.2
  3.5 0.7 copy-start.3
  4.2 0.7 copy-start.4
  4.8 0.7 copy-start.5
  5.5 0.7 copy-start.6
  100.4 80.3 %copy-start.7 = (f32[2,768,384]{2,1,0:T(8,128)S(1)}, f32[2,768,384]{2,1,0:T(8,128)}, u32[]{:S(2)}) copy-start(f32[2,768,384]{2,1,0:T(8,128)} %constant.21) | copy-start | bytes 7077892
  184.3 16.5 %all-to-all-start.2 = ((f32[64,6,8,1]{2,3,1,0:T(1,128)}), f32[64,6,8,1]{2,3,1,0:T(1,128)S(1)}, u32[]{:S(2)}, u32[]{:S(2)}) async-start(f32[64,6,8,1]{2,3,1,0:T(1,128)} %copy.46), calls=%async_computation.2 | async-start | bytes 393216 | tf_op jit(solution)/shard_map/all_to_all | solution.py:292

commit v2 on v1

--- a/solution.py
+++ b/solution.py
@@ -42,12 +42,13 @@
 
 def step_kernel(
     count_z, count_x,
-    fields_ref, material_ref, mask_ref, eps_ref, kerr_ref, pulse_ref, turn_ref,
+    fields_hbm, material_hbm, mask_hbm, eps_hbm, kerr_hbm,
     state, spec,
+    material_ref, mask_ref, eps_ref, kerr_ref, pulse_ref, turn_ref, load_sem,
     eps_v, kerr_v, src_v, fac_v,
-    rows_e, rows_h, rows_top, corner_s,
-    in_xe, in_xh, in_ze, in_zh, in_c,
-    send_sem, recv_sem,
+    rows_e, rows_h, rows_top, corner_s, mix,
+    in_xe, in_xr, in_xh, in_ze, in_zh, in_c,
+    send_sem, recv_sem, corner_send, corner_recv,
 ):
     wide = state.shape[1]
     span = state.shape[3]
@@ -65,11 +66,22 @@
         (has_lx, to_lx), (has_hx, to_hx), (has_lz, to_lz), (has_hz, to_hz), (has_a, to_a), (has_b, to_b)
     )
 
+    loads = [
+        pltpu.make_async_copy(source, there, load_sem.at[i])
+        for i, (source, there) in enumerate((
+            (material_hbm, material_ref), (mask_hbm, mask_ref), (eps_hbm, eps_ref), (kerr_hbm, kerr_ref),
+            (fields_hbm, state),
+        ))
+    ]
+    for item in loads:
+        item.start()
     in_xe[...] = jnp.zeros_like(in_xe)
     in_xh[...] = jnp.zeros_like(in_xh)
     in_ze[...] = jnp.zeros_like(in_ze)
     in_zh[...] = jnp.zeros_like(in_zh)
+    in_xr[...] = jnp.zeros_like(in_xr)
     in_c[...] = jnp.zeros_like(in_c)
+    mix[...] = jnp.zeros_like(mix)
 
     barrier = pltpu.get_barrier_semaphore()
     for has, target in neighbours:
@@ -77,6 +89,12 @@
         def _():
             pl.semaphore_signal(barrier, inc=1, device_id=target, device_id_type=MESH)
 
+    for n in range(STEPS):
+        pulse_ref[n] = jnp.float32(pulses()[n])
+        for i in range(4):
+            turn_ref[4 * n + i] = jnp.float32(turns()[n, i])
+    for item in loads:
+        item.wait()
     material = material_ref[...]
     eps, kerr = jnp.zeros(material.shape, jnp.float32), jnp.zeros(material.shape, jnp.float32)
     for level in range(eps_ref.shape[0]):
@@ -85,7 +103,6 @@
     eps_v[...] = eps
     kerr_v[...] = kerr
     src_v[...] = mask_ref[...].astype(jnp.float32)
-    state[...] = fields_ref[...]
     spec[...] = jnp.zeros_like(spec)
 
     pl.semaphore_wait(barrier, sum(jnp.where(has, 1, 0) for has, _ in neighbours))
@@ -110,6 +127,24 @@
     def wide_row(r):
         return jnp.broadcast_to(r, (8, span))
 
+    def prev_row(r):
+        return jnp.where(first_col[0:1], 0.0, pltpu.roll(r, 1, 1))
+
+    def corner(when, place):
+        return pltpu.make_async_remote_copy(
+            src_ref=corner_s.at[lax.rem(when, 2), place], dst_ref=in_c.at[lax.rem(when, 4), place],
+            send_sem=corner_send.at[lax.rem(when, 2), place], recv_sem=corner_recv.at[lax.rem(when, 4), place],
+            device_id=(to_a, to_b)[place], device_id_type=MESH,
+        )
+
+    corner_s[...] = jnp.zeros_like(corner_s)
+    corner_s[0, 0, 0:1, :] = state[0, last, 0:1, :]
+    corner_s[0, 1, 0:1, :] = state[2, 0, 7:8, :]
+    for place, has in ((0, has_a), (1, has_b)):
+        @pl.when(has)
+        def _():
+            corner(0, place).start()
+
     def one_step(n, carry):
         slot = lax.rem(n, 2)
 
@@ -122,12 +157,12 @@
         for x in range(wide):
             rows_e[0, x : x + 1, :] = state[0, x, 0:1, :]
             rows_e[1, x : x + 1, :] = state[1, x, 0:1, :]
-        corner_s[0:1, :] = state[2, 0, 7:8, :]
+        rows_e[0, wide : wide + 1, :] = state[2, 0, 0:1, :]
+        rows_e[1, wide : wide + 1, :] = state[2, 0, 0:1, :]
         out_lx = copy(0, state.at[1:3, 0], to_lx, in_xe.at[slot], 0)
         out_lz = copy(1, rows_e, to_lz, in_ze.at[slot], 1)
-        out_a = copy(2, rows_e.at[0, last : last + 1], to_a, in_c.at[slot, 0], 2)
-        out_b = copy(3, corner_s, to_b, in_c.at[slot, 1], 3)
-        for has, item in ((has_a, out_a), (has_b, out_b), (has_lx, out_lx), (has_lz, out_lz)):
+        out_rx = copy(2, rows_e.at[0, 0:1], to_lx, in_xr.at[slot], 2)
+        for has, item in ((has_lx, out_lx), (has_lz, out_lz), (has_lx, out_rx)):
             @pl.when(has)
             def _():
                 item.start()
@@ -146,8 +181,8 @@
             state[5, x] = hz
             rows_h[0, x : x + 1, :] = hx[7:8, :]
             rows_h[1, x : x + 1, :] = hy[7:8, :]
-        out_hx = copy(4, state.at[4:6, last], to_hx, in_xh.at[slot], 4)
-        out_hz = copy(5, rows_h, to_hz, in_zh.at[slot], 5)
+        out_hx = copy(3, state.at[4:6, last], to_hx, in_xh.at[slot], 3)
+        out_hz = copy(4, rows_h, to_hz, in_zh.at[slot], 4)
         for has, item in ((has_hz, out_hz), (has_hx, out_hx)):
             @pl.when(has)
             def _():
@@ -157,34 +192,54 @@
             ex, ey, ez = state[0, x], state[1, x], state[2, x]
             fac_v[x] = s / (eps_v[x] + kerr_v[x] * (ex * ex + ey * ey + ez * ez))
 
-        for has, sem, there in (
-            (has_hx, 0, in_xe), (has_lx, 4, in_xh), (has_hz, 1, in_ze), (has_lz, 5, in_zh),
+        pulse = pulse_ref[n]
+        ahead = n + 1
+        side = lax.rem(ahead, 2)
+        corner_s[side, 0, 0:1, :] = (
+            state[0, last, 0:1, :]
+            + fac_v[last, 0:1, :] * (state[5, last, 0:1, :] - prev_row(state[5, last, 0:1, :]) - state[4, last, 0:1, :])
+            + src_v[last, 0:1, :] * pulse
+        )
+        corner_s[side, 0, 1:2, :] = fac_v[last, 0:1, :]
+        corner_s[side, 1, 0:1, :] = state[2, 0, 7:8, :] + fac_v[0, 7:8, :] * (
+            state[4, 0, 7:8, :] - (state[3, 0, 7:8, :] - prev_row(state[3, 0, 7:8, :]))
+        )
+        corner_s[side, 1, 1:2, :] = fac_v[0, 7:8, :]
+        for place, has in ((0, has_a), (1, has_b)):
+            @pl.when(has & (ahead < STEPS))
+            def _():
+                corner(ahead, place).start()
+
+        for has, index, there in (
+            (has_hx, 0, in_xe), (has_lx, 3, in_xh), (has_hz, 1, in_ze), (has_lz, 4, in_zh), (has_hx, 2, in_xr),
         ):
             @pl.when(has)
             def _():
-                pltpu.make_async_remote_copy(
-                    src_ref=there.at[slot], dst_ref=there.at[slot], send_sem=send_sem.at[sem],
-                    recv_sem=recv_sem.at[slot, sem], device_id=to_lx, device_id_type=MESH,
-                ).wait_recv()
-        for has, sem, place in ((has_b, 2, 0), (has_a, 3, 1)):
-            @pl.when(has)
-            def _():
-                pltpu.make_async_remote_copy(
-                    src_ref=in_c.at[slot, place], dst_ref=in_c.at[slot, place], send_sem=send_sem.at[sem],
-                    recv_sem=recv_sem.at[slot, sem], device_id=to_lx, device_id_type=MESH,
-                ).wait_recv()
+                copy(index, there.at[slot], to_lx, there.at[slot], index).wait_recv()
         for has, item in (
-            (has_lx, out_lx), (has_lz, out_lz), (has_a, out_a), (has_b, out_b), (has_hx, out_hx), (has_hz, out_hz)
+            (has_lx, out_lx), (has_lz, out_lz), (has_lx, out_rx), (has_hx, out_hx), (has_hz, out_hz)
         ):
             @pl.when(has)
             def _():
                 item.wait_send()
+        for place, has_to, has_from in ((0, has_a, has_b), (1, has_b, has_a)):
+            @pl.when(has_from)
+            def _():
+                corner(n, place).wait_recv()
+
+            @pl.when(has_to)
+            def _():
+                corner(n, place).wait_send()
+        here = lax.rem(n, 4)
+        corner_ex = in_c[here, 0, 0:1, :] + in_c[here, 0, 1:2, :] * mix[0:1, :]
+        corner_ez = in_c[here, 1, 0:1, :] + in_c[here, 1, 1:2, :] * mix[1:2, :]
 
         ex, ey, ez = state[0, 0], state[1, 0], state[2, 0]
-        corner_x = jnp.where(top_row, wide_row(in_c[slot, 0]), 0.0)
+        corner_x = jnp.where(top_row, wide_row(corner_ex), 0.0)
         before_y = keep_lx * (in_xh[slot, 0] + s * ez - s * corner_x)
         before_z = keep_lx * (in_xh[slot, 1] - s * ey)
-        pulse = pulse_ref[n]
+        face = in_ze[slot, 1, 0:1, :]
+        mix[0:1, :] = before_y[7:8, :] - s * (face - prev_row(face)) - s * in_ze[slot, 0, wide : wide + 1, :]
         for x in range(wide):
             ex, ey, ez = state[0, x], state[1, x], state[2, x]
             above_x = wide_row(in_ze[slot, 0, x : x + 1, :])
@@ -197,7 +252,9 @@
             if x == last:
                 hy = hy + s * in_xe[slot, 1]
                 hz = hz - s * in_xe[slot, 0]
-                below_y = below_y + s * wide_row(in_c[slot, 1])
+                below_y = below_y + s * wide_row(corner_ez)
+                face = in_xe[slot, 0, 0:1, :]
+                mix[1:2, :] = -below_y[0:1, :] - s * in_xr[slot] - s * (face - prev_row(face))
             down_x = jnp.where(first_row, keep_lz * below_x, pltpu.roll(hx, 1, 0))
             down_y = jnp.where(first_row, keep_lz * below_y, pltpu.roll(hy, 1, 0))
             fac = fac_v[x]
@@ -216,7 +273,7 @@
                 rows_top[1, x : x + 1, :] = state[1, x, 7:8, :]
             for f in range(2):
                 for part in range(2):
-                    weight = turn_ref[n, 2 * f + part]
+                    weight = turn_ref[4 * n + 2 * f + part]
                     for c in range(2):
                         spec[4 * f + 2 * c + part] += weight * rows_top[c]
 
@@ -228,7 +285,6 @@
 def march(count_z, count_x, fields, material, mask, eps_table, kerr_table):
     _, wide, deep, span = fields.shape
     vmem = pl.BlockSpec(memory_space=pltpu.VMEM)
-    smem = pl.BlockSpec(memory_space=pltpu.SMEM)
     f32 = jnp.float32
     return pl.pallas_call(
         functools.partial(step_kernel, count_z, count_x),
@@ -236,30 +292,41 @@
             jax.ShapeDtypeStruct(fields.shape, f32),
             jax.ShapeDtypeStruct((8, wide, span), f32),
         ),
-        in_specs=[vmem, vmem, vmem, smem, smem, smem, smem],
+        in_specs=[pl.BlockSpec(memory_space=pl.ANY)] * 5,
         out_specs=(vmem, vmem),
         scratch_shapes=[
+            pltpu.VMEM((wide, deep, span), jnp.int32),
+            pltpu.VMEM((wide, deep, span), jnp.int32),
+            pltpu.SMEM(eps_table.shape, f32),
+            pltpu.SMEM(kerr_table.shape, f32),
+            pltpu.SMEM((STEPS,), f32),
+            pltpu.SMEM((4 * STEPS,), f32),
+            pltpu.SemaphoreType.DMA((5,)),
             pltpu.VMEM((wide, deep, span), f32),
             pltpu.VMEM((wide, deep, span), f32),
             pltpu.VMEM((wide, deep, span), f32),
             pltpu.VMEM((wide, deep, span), f32),
+            pltpu.VMEM((2, wide + 1, span), f32),
             pltpu.VMEM((2, wide, span), f32),
             pltpu.VMEM((2, wide, span), f32),
-            pltpu.VMEM((2, wide, span), f32),
-            pltpu.VMEM((1, span), f32),
+            pltpu.VMEM((2, 2, 2, span), f32),
+            pltpu.VMEM((2, span), f32),
             pltpu.VMEM((2, 2, deep, span), f32),
+            pltpu.VMEM((2, 1, span), f32),
             pltpu.VMEM((2, 2, deep, span), f32),
+            pltpu.VMEM((2, 2, wide + 1, span), f32),
             pltpu.VMEM((2, 2, wide, span), f32),
-            pltpu.VMEM((2, 2, wide, span), f32),
-            pltpu.VMEM((2, 2, 1, span), f32),
-            pltpu.SemaphoreType.DMA((6,)),
-            pltpu.SemaphoreType.DMA((2, 6)),
+            pltpu.VMEM((4, 2, 2, span), f32),
+            pltpu.SemaphoreType.DMA((5,)),
+            pltpu.SemaphoreType.DMA((2, 5)),
+            pltpu.SemaphoreType.DMA((2, 2)),
+            pltpu.SemaphoreType.DMA((4, 2)),
         ],
         compiler_params=pltpu.CompilerParams(
-            collective_id=1, has_side_effects=True, vmem_limit_bytes=32 * 1024 * 1024
+            collective_id=1, has_side_effects=True, vmem_limit_bytes=60 * 1024 * 1024
         ),
         name="march",
-    )(fields, material, mask, eps_table, kerr_table, jnp.asarray(pulses()), jnp.asarray(turns()))
+    )(fields, material, mask, eps_table, kerr_table)
 
 
 def local(fields, material, source_mask, eps_table, kerr_table):

time: 203 us -> 180 us (0.89)
  blocking collectives: 73.2 us -> 60.2 us
  local copies, waits for them, and re-layouts: 9.8 us -> 4.31 us
  Pallas kernels: 94.3 us -> 89.8 us
    all_to_all x1, blocking collectives: 51.9 us -> 38 us  [local(): v = lax.all_to_all(v, 'lat', 0, 0)]
    unnamed x19 -> x7, local copies, waits for them, and re-layouts: 6.57 us -> 1.07 us
    pallas_call x1, Pallas kernels: 94.3 us -> 89.8 us  [march(): pl.pallas_call(functools.partial(step_kernel, count_z, count_x), out_shap...]
where the time goes in v2:
time: 180 us; the launch traced here: 179 us
  Pallas kernels  89.8 us (50%)
  blocking collectives  60.2 us (33%)
  waiting for transfers between devices  10 us (6%)
  matrix products  6.83 us (4%)
  starting transfers between devices  6.52 us (4%)
  local copies, waits for them, and re-layouts  4.31 us (2%)
    pallas_call x1, Pallas kernels, march(): pl.pallas_call(functools.partial(step_kernel, count_z, count_x), out_shap...  89.8 us
    all_to_all x1, blocking collectives, local(): v = lax.all_to_all(v, 'lat', 0, 0)  38 us
    all_to_all x1, blocking collectives, local(): v = lax.all_to_all(v, 'depth', 0, 0)[count_z - 1]  22.2 us
    all_to_all x1, waiting for transfers between devices, local(): w = lax.all_to_all(w, 'lat', 0, 0)  10 us
    all_to_all x1, starting transfers between devices, local(): w = lax.all_to_all(w, 'lat', 0, 0)  6.52 us
    dot_general x1, matrix products, local(): prod = jnp.einsum('fcpxy,fyk->fcpxk', spec, both, precision=HIGHEST)  4.77 us
  transfers between devices with their start and end apart: 1, of which 1 were waited for; matrix products, arithmetic and copies ran while one was open for 0% of the time, Pallas kernels for 0%

profile of v2, /device:TPU:1, one launch (start us, length us, event | category | flops | bytes accessed | tf_op | source)
XLA Modules:
  0.0 179.4 jit_solution(17600246802285057512)
XLA Ops:
  0.6 89.8 %march.1 = (f32[6,6,8,512]{3,2,1,0:T(8,128)}, f32[8,6,512]{2,1,0:T(8,128)}) custom-call(f32[6,6,8,512]{3,2,1,0:T(8,128)} %fields_hbm.1, s32[6,8,512]{2,1,0:T(8,128)} %material_hbm.1, s32[6,8,512]{2,1,0:T(8,128)} %mask_hbm.1, f32[4]{0:T(128)} %eps_hbm.1, f32[4]{0:T(128)} %kerr_hbm.1), custom_call_target="tpu_custom_call" | custom-call | tf_op jit(solution)/shard_map/march/pallas_call | solution.py:289
  90.5 0.0 copy-start
  90.5 4.8 %fusion.7 = f32[2,2,2,6,1024]{4,3,2,1,0:T(8,128)S(1)} fusion(f32[2,2,2,6,512]{4,3,2,1,0:T(8,128)} %bitcast.66, f32[2,512,1024,1,1]{2,1,4,3,0:T(8,128)} %constant.17), kind=kOutput, calls=%fused_computation.16 | convolution fusion | flops 301989888 | bytes 4489216 | tf_op jit(solution)/shard_map/fcpxy,fyk->fcpxk/dot_general | solution.py:339
  95.2 0.0 copy-start.1
  95.3 0.1 reshape.105
  95.5 0.2 reshape.111
  95.6 22.2 %all_to_all.15 = f32[8,1,3072]{2,1,0:T(1,128)S(1)} all-to-all(f32[8,1,3072]{2,1,0:T(1,128)S(1)} %reshape.111), channel_id=1, replica_groups=mesh['depth'=8,'lat'=64] {'depth'}, dimensions={0} | all-to-all | bytes 196608 | tf_op jit(solution)/shard_map/all_to_all | solution.py:345
  117.8 0.5 broadcast
  118.3 0.9 reduce
  119.2 0.1 reshape.112
  119.3 0.2 copy.38
  119.5 38.0 %all_to_all.16 = f32[64,2,2,2,6,1]{4,3,1,2,5,0:T(2,128)S(1)} all-to-all(f32[64,2,2,2,6,1]{4,3,1,2,5,0:T(2,128)S(1)} %copy.38), channel_id=1, replica_groups=mesh['depth'=8,'lat'=64] {'lat'}, dimensions={0} | all-to-all | bytes 24576 | tf_op jit(solution)/shard_map/all_to_all | solution.py:348
  157.5 0.1 copy.39
  157.6 0.2 reshape.106
  157.7 0.0 copy-done
  157.8 2.1 %fusion.8 = f32[2,768,4]{1,2,0:T(4,128)S(1)} fusion(f32[2,768,384]{2,1,0:T(8,128)S(1)} %copy-done, f32[2,384,4]{1,2,0:T(4,128)S(1)} %reshape.106), kind=kOutput, calls=%fused_computation.17 | convolution fusion | flops 28311552 | bytes 2396160 | tf_op jit(solution)/shard_map/fix,fxn->fin/dot_general | solution.py:352
  159.9 0.2 reshape.108
  160.1 1.1 copy.44
  161.3 6.5 %all-to-all-start.2 = ((f32[64,6,8,1]{2,3,1,0:T(1,128)}), f32[64,6,8,1]{2,3,1,0:T(1,128)S(1)}, u32[]{:S(2)}, u32[]{:S(2)}) async-start(f32[64,6,8,1]{2,3,1,0:T(1,128)} %copy.44), calls=%async_computation.2 | async-start | bytes 393216 | tf_op jit(solution)/shard_map/all_to_all | solution.py:359
  167.8 10.0 %all-to-all-done.2 = f32[64,6,8,1]{2,3,1,0:T(1,128)S(1)} async-done(((f32[64,6,8,1]{2,3,1,0:T(1,128)}), f32[64,6,8,1]{2,3,1,0:T(1,128)S(1)}, u32[]{:S(2)}, u32[]{:S(2)}) %all-to-all-start.2) | async-done | bytes 12320 | tf_op jit(solution)/shard_map/all_to_all | solution.py:359
  177.8 0.7 copy.45
  178.6 0.0 copy-done.1
  178.6 0.8 copy.54
  (8 shorter events, 0.2 us)
Async XLA Ops:
  90.5 67.3 %copy-start = (f32[2,768,384]{2,1,0:T(8,128)S(1)}, f32[2,768,384]{2,1,0:T(8,128)}, u32[]{:S(2)}) copy-start(f32[2,768,384]{2,1,0:T(8,128)} %constant.15) | copy-start | bytes 7077892
  95.2 83.3 %copy-start.1 = (f32[6,6,8,512]{3,2,1,0:T(8,128)S(1)}, f32[6,6,8,512]{3,2,1,0:T(8,128)}, u32[]{:S(2)}) copy-start(f32[6,6,8,512]{3,2,1,0:T(8,128)} %get-tuple-element.14) | copy-start | bytes 1769476
  161.3 16.5 %all-to-all-start.2 = ((f32[64,6,8,1]{2,3,1,0:T(1,128)}), f32[64,6,8,1]{2,3,1,0:T(1,128)S(1)}, u32[]{:S(2)}, u32[]{:S(2)}) async-start(f32[64,6,8,1]{2,3,1,0:T(1,128)} %copy.44), calls=%async_computation.2 | async-start | bytes 393216 | tf_op jit(solution)/shard_map/all_to_all | solution.py:359

commit v3 on v2

--- a/solution.py
+++ b/solution.py
@@ -13,7 +13,6 @@
 COURANT = 0.55
 OMEGAS = (0.9, 1.3)
 QUARTERS = (3, 5)
-HIGHEST = lax.Precision.HIGHEST
 MESH = pl.DeviceIdType.MESH
 
 
@@ -30,20 +29,29 @@
     return np.asarray(np.stack(parts, axis=1), np.float32)
 
 
-def chirp(length):
+def split(table):
+    high = table.astype(jnp.bfloat16)
+    return high, (table - high.astype(np.float32)).astype(jnp.bfloat16)
+
+
+def chirp(length, run):
     gap = np.arange(length)[:, None] - np.arange(length)[None, :]
-    reals, imags = [], []
+    padded = -(-run // 8) * 8
+    tables = []
     for quarter in QUARTERS:
         phase = (quarter * gap * gap % (8 * length)) * (math.pi / (4.0 * length))
-        reals.append(np.cos(phase) / math.sqrt(length))
-        imags.append(np.sin(phase) / math.sqrt(length))
-    return np.asarray(np.stack(reals), np.float32), np.asarray(np.stack(imags), np.float32)
+        table = np.stack([np.cos(phase), np.sin(phase)], axis=1) / math.sqrt(length)
+        table = table.reshape(length // run, run, 2, length // run, run)
+        table = np.pad(table, ((0, 0), (0, padded - run), (0, 0), (0, 0), (0, padded - run)))
+        tables.append(table.reshape(length // run * padded, 2 * (length // run) * padded))
+    return split(np.asarray(np.stack(tables), np.float32))
 
 
 def step_kernel(
     count_z, count_x,
-    fields_hbm, material_hbm, mask_hbm, eps_hbm, kerr_hbm,
-    state, spec,
+    fields_hbm, material_hbm, mask_hbm, eps_hbm, kerr_hbm, col_high_hbm, col_low_hbm, row_high_hbm, row_low_hbm,
+    state, image,
+    spec, col_high, col_low, row_high, row_low, table_sem, planes, out_a, in_a, out_b, in_b, tail_send, tail_recv,
     material_ref, mask_ref, eps_ref, kerr_ref, pulse_ref, turn_ref, load_sem,
     eps_v, kerr_v, src_v, fac_v,
     rows_e, rows_h, rows_top, corner_s, mix,
@@ -89,6 +97,34 @@
         def _():
             pl.semaphore_signal(barrier, inc=1, device_id=target, device_id_type=MESH)
 
+    exit_z = count_z - 1
+    at_exit = pos_z == exit_z
+    group = count_x // count_z
+    for j in range(group):
+        sender = pos_z * group + j
+        @pl.when(jnp.logical_not(at_exit & (sender == pos_x)))
+        def _():
+            pl.semaphore_signal(barrier, inc=1, device_id=(exit_z, sender), device_id_type=MESH)
+
+    tables = [
+        pltpu.make_async_copy(source, there, table_sem.at[i])
+        for i, (source, there) in enumerate((
+            (col_high_hbm, col_high), (col_low_hbm, col_low), (row_high_hbm, row_high), (row_low_hbm, row_low)
+        ))
+    ]
+
+    @pl.when(at_exit)
+    def _():
+        def greet(i, carry):
+            pl.semaphore_signal(
+                barrier, inc=1, device_id=(exit_z, lax.rem(pos_x + i, count_x)), device_id_type=MESH
+            )
+            return carry
+
+        lax.fori_loop(1, count_x, greet, 0)
+        for item in tables:
+            item.start()
+
     for n in range(STEPS):
         pulse_ref[n] = jnp.float32(pulses()[n])
         for i in range(4):
@@ -104,8 +140,12 @@
     kerr_v[...] = kerr
     src_v[...] = mask_ref[...].astype(jnp.float32)
     spec[...] = jnp.zeros_like(spec)
-
-    pl.semaphore_wait(barrier, sum(jnp.where(has, 1, 0) for has, _ in neighbours))
+    rows_top[...] = jnp.zeros_like(rows_top)
+
+    target_z = pos_x // group
+    greeted = sum(jnp.where(has, 1, 0) for has, _ in neighbours)
+    greeted += jnp.where(at_exit, 2 * count_x - 1 - jnp.where(target_z == exit_z, 1, 0), 0)
+    pl.semaphore_wait(barrier, greeted)
 
     row = lax.broadcasted_iota(jnp.int32, (8, span), 0)
     col = lax.broadcasted_iota(jnp.int32, (8, span), 1)
@@ -266,7 +306,7 @@
             state[5, x] = hz
             before_y, before_z = hy, hz
 
-        @pl.when(pos_z == count_z - 1)
+        @pl.when(at_exit)
         def _():
             for x in range(wide):
                 rows_top[0, x : x + 1, :] = state[0, x, 7:8, :]
@@ -281,20 +321,156 @@
 
     lax.fori_loop(0, STEPS, one_step, 0)
 
+    lane_group = lax.broadcasted_iota(jnp.int32, (8, 128), 1) // 8
+    half = planes.shape[1] // 2
+
+    def place_plane(index, value, lanes):
+        f, c, part = index // 4, index // 2 % 2, index % 2
+        base = 32 * f + 16 * c
+        if part == 0:
+            planes[base : base + 8, pl.ds(lanes, value.shape[1])] = value
+            planes[base + 8 : base + 16, pl.ds(half + lanes, value.shape[1])] = value
+        else:
+            planes[base : base + 8, pl.ds(half + lanes, value.shape[1])] = -value
+            planes[base + 8 : base + 16, pl.ds(lanes, value.shape[1])] = value
+
+    def transform(high, low, result):
+        total = None
+        for f in range(2):
+            value = planes[...]
+            mine = lax.broadcasted_iota(jnp.int32, value.shape, 0) // 32 == f
+            value = jnp.where(mine, value, 0.0)
+            upper = value.astype(jnp.bfloat16)
+            lower = (value - upper.astype(jnp.float32)).astype(jnp.bfloat16)
+            right = jnp.concatenate([upper, lower], axis=0)
+            dims = (((1,), (1,)), ((), ()))
+            first = lax.dot_general(high[f], right, dims, preferred_element_type=jnp.float32)
+            second = lax.dot_general(low[f], right, dims, preferred_element_type=jnp.float32)
+            part = first + pltpu.roll(first, 64, 1) + second
+            total = part if total is None else total + part
+        result[...] = total
+
+    def tile(ref, index):
+        return ref.at[pl.ds(pl.multiple_of(8 * index, 8), 8), :]
+
+    @pl.when(at_exit)
+    def _():
+        for item in tables:
+            item.wait()
+        for index in range(8):
+            place_plane(index, spec[index], 0)
+        transform(col_high, col_low, out_a)
+
+        def send_a(i, carry):
+            peer = lax.rem(pos_x + i, count_x)
+            pltpu.make_async_remote_copy(
+                src_ref=tile(out_a, peer), dst_ref=in_a.at[pos_x], send_sem=tail_send.at[0],
+                recv_sem=tail_recv.at[0], device_id=(exit_z, peer), device_id_type=MESH,
+            ).start()
+            return carry
+
+        lax.fori_loop(1, count_x, send_a, 0)
+        in_a[pos_x] = out_a[pl.ds(pl.multiple_of(8 * pos_x, 8), 8), :]
+        others = in_a.at[pl.ds(0, count_x - 1)]
+        whole = pltpu.make_async_remote_copy(
+            src_ref=others, dst_ref=others, send_sem=tail_send.at[0], recv_sem=tail_recv.at[0],
+            device_id=(exit_z, pos_x), device_id_type=MESH,
+        )
+        whole.wait_recv()
+        whole.wait_send()
+        for block in range(count_x // 16):
+            values = [in_a[16 * block + j] for j in range(16)]
+            for index in range(8):
+                lined = jnp.zeros((8, 128), jnp.float32)
+                for j in range(16):
+                    moved = pltpu.roll(values[j], (8 * (j - index)) % 128, 1) if j != index else values[j]
+                    lined = jnp.where(lane_group == j, moved, lined)
+                place_plane(index, lined, 128 * block)
+        transform(row_high, row_low, out_b)
+        mine = lax.rem(pos_x, group)
+
+        def send_b(i, carry):
+            peer = lax.rem(pos_x + i, count_x)
+            pltpu.make_async_remote_copy(
+                src_ref=tile(out_b, peer), dst_ref=in_b.at[mine], send_sem=tail_send.at[1],
+                recv_sem=tail_recv.at[1], device_id=(target_z, peer), device_id_type=MESH,
+            ).start()
+            return carry
+
+        lax.fori_loop(1, count_x, send_b, 0)
+
+        @pl.when(target_z != exit_z)
+        def _():
+            send_b(0, 0)
+
+        @pl.when(target_z == exit_z)
+        def _():
+            in_b[mine] = out_b[pl.ds(pl.multiple_of(8 * pos_x, 8), 8), :]
+
+    def arrived(number):
+        return pltpu.make_async_remote_copy(
+            src_ref=in_a.at[pl.ds(0, number)], dst_ref=in_b.at[pl.ds(0, number)], send_sem=tail_send.at[1],
+            recv_sem=tail_recv.at[1], device_id=(exit_z, pos_x), device_id_type=MESH,
+        )
+
+    own = at_exit & (target_z == exit_z)
+
+    @pl.when(own)
+    def _():
+        arrived(group - 1).wait_recv()
+
+    @pl.when(jnp.logical_not(own))
+    def _():
+        arrived(group).wait_recv()
+
+    columns = image.shape[2]
+    values = [in_b[j] for j in range(group)]
+    for index in range(8):
+        lined = jnp.zeros((8, 128), jnp.float32)
+        for j in range(group):
+            moved = pltpu.roll(values[j], (8 * (j - index)) % 128, 1) if j != index else values[j]
+            lined = jnp.where(lane_group == j, moved, lined)
+        image[:, index, :] = lined[:wide, :columns]
+
+    def sent(number):
+        return pltpu.make_async_remote_copy(
+            src_ref=in_a.at[pl.ds(0, number)], dst_ref=in_a.at[pl.ds(0, number)], send_sem=tail_send.at[1],
+            recv_sem=tail_recv.at[1], device_id=(exit_z, pos_x), device_id_type=MESH,
+        )
+
+    @pl.when(own)
+    def _():
+        sent(count_x - 1).wait_send()
+
+    @pl.when(at_exit & jnp.logical_not(own))
+    def _():
+        sent(count_x).wait_send()
+
 
 def march(count_z, count_x, fields, material, mask, eps_table, kerr_table):
     _, wide, deep, span = fields.shape
     vmem = pl.BlockSpec(memory_space=pltpu.VMEM)
     f32 = jnp.float32
+    tables = chirp(span, span) + chirp(count_x * wide, wide)
     return pl.pallas_call(
         functools.partial(step_kernel, count_z, count_x),
         out_shape=(
             jax.ShapeDtypeStruct(fields.shape, f32),
-            jax.ShapeDtypeStruct((8, wide, span), f32),
+            jax.ShapeDtypeStruct((wide, 8, span // count_z), f32),
         ),
-        in_specs=[pl.BlockSpec(memory_space=pl.ANY)] * 5,
+        in_specs=[pl.BlockSpec(memory_space=pl.ANY)] * 9,
         out_specs=(vmem, vmem),
         scratch_shapes=[
+            pltpu.VMEM((8, 8, span), f32),
+            *(pltpu.VMEM(table.shape, jnp.bfloat16) for table in tables),
+            pltpu.SemaphoreType.DMA((4,)),
+            pltpu.VMEM((64, 2 * max(span, 8 * count_x)), f32),
+            pltpu.VMEM((span, 128), f32),
+            pltpu.VMEM((count_x, 8, 128), f32),
+            pltpu.VMEM((8 * count_x, 128), f32),
+            pltpu.VMEM((count_x // count_z, 8, 128), f32),
+            pltpu.SemaphoreType.DMA((2,)),
+            pltpu.SemaphoreType.DMA((2,)),
             pltpu.VMEM((wide, deep, span), jnp.int32),
             pltpu.VMEM((wide, deep, span), jnp.int32),
             pltpu.SMEM(eps_table.shape, f32),
@@ -308,7 +484,7 @@
             pltpu.VMEM((wide, deep, span), f32),
             pltpu.VMEM((2, wide + 1, span), f32),
             pltpu.VMEM((2, wide, span), f32),
-            pltpu.VMEM((2, wide, span), f32),
+            pltpu.VMEM((2, 8, span), f32),
             pltpu.VMEM((2, 2, 2, span), f32),
             pltpu.VMEM((2, span), f32),
             pltpu.VMEM((2, 2, deep, span), f32),
@@ -326,39 +502,12 @@
             collective_id=1, has_side_effects=True, vmem_limit_bytes=60 * 1024 * 1024
         ),
         name="march",
-    )(fields, material, mask, eps_table, kerr_table)
+    )(fields, material, mask, eps_table, kerr_table, *(jnp.asarray(table) for table in tables))
 
 
 def local(fields, material, source_mask, eps_table, kerr_table):
-    _, wide, deep, span = fields.shape
     count_x, count_z = lax.axis_size("lat"), lax.axis_size("depth")
-    state, spec = march(count_z, count_x, fields, material, source_mask, eps_table, kerr_table)
-    spec = spec.reshape(2, 2, 2, wide, span)
-    y_real, y_imag = (jnp.asarray(part) for part in chirp(span))
-    both = jnp.concatenate([y_real, y_imag], axis=2)
-    prod = jnp.einsum("fcpxy,fyk->fcpxk", spec, both, precision=HIGHEST)
-    v_real = prod[:, :, 0, :, :span] - prod[:, :, 1, :, span:]
-    v_imag = prod[:, :, 0, :, span:] + prod[:, :, 1, :, :span]
-    v = jnp.stack([v_real, v_imag])
-    cols = span // count_z
-    v = v.reshape(8 * wide, count_z, cols).transpose(1, 0, 2)
-    v = lax.all_to_all(v, "depth", 0, 0)[count_z - 1]
-    per = cols // count_x
-    v = v.reshape(2, 2, 2, wide, count_x, per).transpose(4, 0, 1, 2, 3, 5)
-    v = lax.all_to_all(v, "lat", 0, 0)
-    v = v.transpose(2, 0, 4, 1, 3, 5).reshape(2, count_x * wide, 2 * 2 * per)
-    x_real, x_imag = (jnp.asarray(part) for part in chirp(count_x * wide))
-    both = jnp.concatenate([x_real, x_imag], axis=1)
-    w = jnp.einsum("fix,fxn->fin", both, v, precision=HIGHEST)
-    total = count_x * wide
-    w = w.reshape(2, 2, total, 2, 2, per)
-    w_real = w[:, 0, :, 0] - w[:, 1, :, 1]
-    w_imag = w[:, 0, :, 1] + w[:, 1, :, 0]
-    w = jnp.stack([w_real, w_imag], axis=3)
-    w = w.transpose(1, 0, 2, 3, 4).reshape(count_x, wide, 8, per)
-    w = lax.all_to_all(w, "lat", 0, 0)
-    image = w.transpose(1, 2, 0, 3).reshape(wide, 8, cols)
-    return state, image
+    return march(count_z, count_x, fields, material, source_mask, eps_table, kerr_table)
 
 
 def solution(mesh):

time: 180 us -> 135 us (0.75)
  blocking collectives: 60.2 us -> 0 us
  Pallas kernels: 89.8 us -> 131 us
  waiting for transfers between devices: 10 us -> 0 us
  matrix products: 6.83 us -> 0 us
  starting transfers between devices: 6.52 us -> 0 us
    all_to_all x2 -> x0, blocking collectives: 60.2 us -> none  [the longest x1 38 us: local(): v = lax.all_to_all(v, 'lat', 0, 0)]
    pallas_call x1, Pallas kernels: 89.8 us -> 131 us  [march(): pl.pallas_call(functools.partial(step_kernel, count_z, count_x), out_shap...]
    all_to_all x1 -> x0, waiting for transfers between devices: 10 us -> none  [local(): w = lax.all_to_all(w, 'lat', 0, 0)]
    dot_general x2 -> x0, matrix products: 6.83 us -> none  [the longest x1 4.77 us: local(): prod = jnp.einsum('fcpxy,fyk->fcpxk', spec, both, precision=HIGHEST)]
    all_to_all x1 -> x0, starting transfers between devices: 6.52 us -> none  [local(): w = lax.all_to_all(w, 'lat', 0, 0)]
    unnamed x7 -> x2, local copies, waits for them, and re-layouts: 1.07 us -> 3.28 us
  transfers between devices with their start and end apart: 1 -> 0, of which waited for: 1 -> 0; matrix products, arithmetic and copies ran while one was open for 0% -> 0% of each run, Pallas kernels for 0% -> 0%
where the time goes in v3:
time: 135 us
  Pallas kernels  131 us (97%)
  local copies, waits for them, and re-layouts  3.28 us (2%)
    pallas_call x1, Pallas kernels, march(): pl.pallas_call(functools.partial(step_kernel, count_z, count_x), out_shap...  131 us
    unnamed x2, local copies, waits for them, and re-layouts  3.28 us

profile of v3, /device:TPU:1, one launch (start us, length us, event | category | flops | bytes accessed | tf_op | source)
XLA Modules:
  0.0 134.8 jit_solution(13095482733516426749)
XLA Ops:
  0.6 130.9 %march.1 = (f32[6,6,8,512]{3,2,1,0:T(8,128)}, f32[6,8,64]{2,1,0:T(8,128)}) custom-call(f32[6,6,8,512]{3,2,1,0:T(8,128)} %fields_hbm.1, s32[6,8,512]{2,1,0:T(8,128)} %material_hbm.1, s32[6,8,512]{2,1,0:T(8,128)} %mask_hbm.1, f32[4]{0:T(128)} %eps_hbm.1, f32[4]{0:T(128)} %kerr_hbm.1, bf16[2,512,1024]{2,1,0:T(8,128)(2,1)} %constant.8.clone.col_high_hbm, ...), custom_call_target="tpu_custom_call" | custom-call | tf_op jit(solution)/shard_map/march/pallas_call | solution.py:455
  131.5 1.9 %copy.13 = f32[6,6,8,512]{3,2,1,0:T(8,128)} copy(f32[6,6,8,512]{3,2,1,0:T(8,128)} %get-tuple-element.4) | data formatting | bytes 1179648
  133.5 1.3 copy.14

commit v4 on v3

--- a/solution.py
+++ b/solution.py
@@ -55,8 +55,7 @@
     material_ref, mask_ref, eps_ref, kerr_ref, pulse_ref, turn_ref, load_sem,
     eps_v, kerr_v, src_v, fac_v,
     rows_e, rows_h, rows_top, corner_s, mix,
-    in_xe, in_xr, in_xh, in_ze, in_zh, in_c,
-    send_sem, recv_sem, corner_send, corner_recv,
+    in_all, in_c, send_sem, recv_sem, corner_send, corner_recv,
 ):
     wide = state.shape[1]
     span = state.shape[3]
@@ -65,11 +64,11 @@
     pos_x = lax.axis_index("lat")
     has_lx, has_hx = pos_x > 0, pos_x < count_x - 1
     has_lz, has_hz = pos_z > 0, pos_z < count_z - 1
-    has_a = has_lz & has_hx
-    has_b = has_hz & has_lx
-    to_lx, to_hx = (pos_z, pos_x - 1), (pos_z, pos_x + 1)
-    to_lz, to_hz = (pos_z - 1, pos_x), (pos_z + 1, pos_x)
-    to_a, to_b = (pos_z - 1, pos_x + 1), (pos_z + 1, pos_x - 1)
+    has_a, has_b = has_lz & has_hx, has_hz & has_lx
+    low_x, high_x, low_z, high_z = pos_x - 1, pos_x + 1, pos_z - 1, pos_z + 1
+    to_lx, to_hx = (pos_z, low_x), (pos_z, high_x)
+    to_lz, to_hz = (low_z, pos_x), (high_z, pos_x)
+    to_a, to_b = (low_z, high_x), (high_z, low_x)
     neighbours = (
         (has_lx, to_lx), (has_hx, to_hx), (has_lz, to_lz), (has_hz, to_hz), (has_a, to_a), (has_b, to_b)
     )
@@ -83,13 +82,31 @@
     ]
     for item in loads:
         item.start()
-    in_xe[...] = jnp.zeros_like(in_xe)
-    in_xh[...] = jnp.zeros_like(in_xh)
-    in_ze[...] = jnp.zeros_like(in_ze)
-    in_zh[...] = jnp.zeros_like(in_zh)
-    in_xr[...] = jnp.zeros_like(in_xr)
+    mix[...] = jnp.zeros_like(mix)
+    in_all[...] = jnp.zeros_like(in_all)
     in_c[...] = jnp.zeros_like(in_c)
-    mix[...] = jnp.zeros_like(mix)
+
+    def begin(has, item):
+        @pl.when(has)
+        def _():
+            item.start()
+
+    def for_peers(act):
+        side = 4 if count_x == 64 else 2
+        runs = count_x // (side * side)
+        x, z, y = pos_x // (side * runs), pos_x // side % runs, pos_x % side
+        order = (2, 1, 3, 0) if side == 4 else (1, 0)
+        at_x = [lax.rem(x + far, side) * (side * runs) for far in order]
+        at_y = [lax.rem(y + far, side) for far in order]
+
+        def run(k, carry):
+            at_z = jnp.where(z < runs // 2, runs - 1 - k, k) * side
+            for i in range(side):
+                for j in range(side):
+                    act(at_x[i] + at_z + at_y[j], i == side - 1 and j == side - 1)
+            return carry
+
+        lax.fori_loop(0, runs, run, 0)
 
     barrier = pltpu.get_barrier_semaphore()
     for has, target in neighbours:
@@ -115,20 +132,22 @@
 
     @pl.when(at_exit)
     def _():
-        def greet(i, carry):
-            pl.semaphore_signal(
-                barrier, inc=1, device_id=(exit_z, lax.rem(pos_x + i, count_x)), device_id_type=MESH
-            )
-            return carry
-
-        lax.fori_loop(1, count_x, greet, 0)
+        def greet(peer, may_be_own):
+            def signal():
+                pl.semaphore_signal(barrier, inc=1, device_id=(exit_z, peer), device_id_type=MESH)
+
+            pl.when(peer != pos_x)(signal) if may_be_own else signal()
+
+        for_peers(greet)
         for item in tables:
             item.start()
 
     for n in range(STEPS):
         pulse_ref[n] = jnp.float32(pulses()[n])
         for i in range(4):
-            turn_ref[4 * n + i] = jnp.float32(turns()[n, i])
+            turn_ref[4 * n + 4 + i] = jnp.float32(turns()[n, i])
+    for i in range(4):
+        turn_ref[i] = jnp.float32(0.0)
     for item in loads:
         item.wait()
     material = material_ref[...]
@@ -154,6 +173,8 @@
     s = jnp.float32(COURANT)
     keep_lx = jnp.where(has_lx, 1.0, 0.0).astype(jnp.float32)
     keep_lz = jnp.where(has_lz, 1.0, 0.0).astype(jnp.float32)
+    keep_hx = jnp.where(has_hx, 1.0, 0.0).astype(jnp.float32)
+    keep_hz = jnp.where(has_hz, 1.0, 0.0).astype(jnp.float32)
 
     def next_y(f):
         return jnp.where(top_col, 0.0, pltpu.roll(f, span - 1, 1))
@@ -180,53 +201,89 @@
     corner_s[...] = jnp.zeros_like(corner_s)
     corner_s[0, 0, 0:1, :] = state[0, last, 0:1, :]
     corner_s[0, 1, 0:1, :] = state[2, 0, 7:8, :]
-    for place, has in ((0, has_a), (1, has_b)):
-        @pl.when(has)
+    begin(has_a, corner(0, 0))
+    begin(has_b, corner(0, 1))
+
+    half = wide // 2
+
+    def keep_rows(x, ex, ey, ez):
+        part, place = x // half, x % half
+        rows_e[part, place : place + 1, :] = ex[0:1, :]
+        rows_e[part, half + place : half + place + 1, :] = ey[0:1, :]
+        if x == 0:
+            rows_e[0, 2 * half : 2 * half + 1, :] = ez[0:1, :]
+
+    def advance_h(x):
+        ex, ey, ez = state[0, x], state[1, x], state[2, x]
+        if x < last:
+            ahead_y, ahead_z = state[1, x + 1], state[2, x + 1]
+        else:
+            ahead_y, ahead_z = jnp.zeros_like(ey), jnp.zeros_like(ez)
+        hx = state[3, x] - s * ((next_y(ez) - ez) - (next_z(ey) - ey))
+        hy = state[4, x] - s * ((next_z(ex) - ex) - (ahead_z - ez))
+        hz = state[5, x] - s * ((ahead_y - ey) - (next_y(ex) - ex))
+        state[3, x] = hx
+        state[4, x] = hy
+        state[5, x] = hz
+        part, place = x // half, x % half
+        rows_h[part, place : place + 1, :] = hx[7:8, :]
+        rows_h[part, half + place : half + place + 1, :] = hy[7:8, :]
+
+    def copies(n):
+        slot = lax.rem(n, 2)
+
+        def copy(index, source, target, there):
+            return pltpu.make_async_remote_copy(
+                src_ref=source, dst_ref=there, send_sem=send_sem.at[index], recv_sem=recv_sem.at[slot, index],
+                device_id=target, device_id_type=MESH,
+            )
+
+        first, second = slice(0, 2 * half + 1), slice(0, 2 * half)
+        return {
+            "xe": (copy(0, state.at[1:3, 0], to_lx, in_all.at[slot, 0:2]), has_lx, has_hx),
+            "xr": (copy(1, rows_e.at[0, 0:1], to_lx, in_all.at[slot, 8, 0:1]), has_lx, has_hx),
+            "xh": (copy(2, state.at[4:6, last], to_hx, in_all.at[slot, 2:4]), has_hx, has_lx),
+            "ze0": (copy(3, rows_e.at[0, first], to_lz, in_all.at[slot, 4, first]), has_lz, has_hz),
+            "ze1": (copy(4, rows_e.at[1, second], to_lz, in_all.at[slot, 5, second]), has_lz, has_hz),
+            "zh0": (copy(5, rows_h.at[0, second], to_hz, in_all.at[slot, 6, second]), has_hz, has_lz),
+            "zh1": (copy(6, rows_h.at[1, second], to_hz, in_all.at[slot, 7, second]), has_hz, has_lz),
+        }
+
+    def send(items, *names):
+        for name in names:
+            item, has_to, _ = items[name]
+            begin(has_to, item)
+
+    def receive(items, *names):
+        for name in names:
+            item, _, has_from = items[name]
+            pl.when(has_from)(item.wait_recv)
+
+    def accumulate(n):
+        for x in range(wide):
+            rows_top[0, x : x + 1, :] = state[0, x, 7:8, :]
+            rows_top[1, x : x + 1, :] = state[1, x, 7:8, :]
+        for f in range(2):
+            for part in range(2):
+                weight = turn_ref[4 * n + 2 * f + part]
+                for c in range(2):
+                    spec[4 * f + 2 * c + part] += weight * rows_top[c]
+
+    for x in range(wide):
+        keep_rows(x, state[0, x], state[1, x], state[2, x])
+    started = copies(0)
+    send(started, "ze0", "ze1", "xe", "xr")
+    for x in range(wide):
+        advance_h(x)
+    send(started, "zh0", "zh1", "xh")
+
+    def one_step(n, more):
+        slot = lax.rem(n, 2)
+        now, later = copies(n), copies(n + 1) if more else {}
+
+        @pl.when(at_exit)
         def _():
-            corner(0, place).start()
-
-    def one_step(n, carry):
-        slot = lax.rem(n, 2)
-
-        def copy(index, source, target, there, sem):
-            return pltpu.make_async_remote_copy(
-                src_ref=source, dst_ref=there, send_sem=send_sem.at[index],
-                recv_sem=recv_sem.at[slot, sem], device_id=target, device_id_type=MESH,
-            )
-
-        for x in range(wide):
-            rows_e[0, x : x + 1, :] = state[0, x, 0:1, :]
-            rows_e[1, x : x + 1, :] = state[1, x, 0:1, :]
-        rows_e[0, wide : wide + 1, :] = state[2, 0, 0:1, :]
-        rows_e[1, wide : wide + 1, :] = state[2, 0, 0:1, :]
-        out_lx = copy(0, state.at[1:3, 0], to_lx, in_xe.at[slot], 0)
-        out_lz = copy(1, rows_e, to_lz, in_ze.at[slot], 1)
-        out_rx = copy(2, rows_e.at[0, 0:1], to_lx, in_xr.at[slot], 2)
-        for has, item in ((has_lx, out_lx), (has_lz, out_lz), (has_lx, out_rx)):
-            @pl.when(has)
-            def _():
-                item.start()
-
-        for x in [last] + list(range(last)):
-            ex, ey, ez = state[0, x], state[1, x], state[2, x]
-            if x < last:
-                ahead_y, ahead_z = state[1, x + 1], state[2, x + 1]
-            else:
-                ahead_y, ahead_z = jnp.zeros_like(ey), jnp.zeros_like(ez)
-            hx = state[3, x] - s * ((next_y(ez) - ez) - (next_z(ey) - ey))
-            hy = state[4, x] - s * ((next_z(ex) - ex) - (ahead_z - ez))
-            hz = state[5, x] - s * ((ahead_y - ey) - (next_y(ex) - ex))
-            state[3, x] = hx
-            state[4, x] = hy
-            state[5, x] = hz
-            rows_h[0, x : x + 1, :] = hx[7:8, :]
-            rows_h[1, x : x + 1, :] = hy[7:8, :]
-        out_hx = copy(3, state.at[4:6, last], to_hx, in_xh.at[slot], 3)
-        out_hz = copy(4, rows_h, to_hz, in_zh.at[slot], 4)
-        for has, item in ((has_hz, out_hz), (has_hx, out_hx)):
-            @pl.when(has)
-            def _():
-                item.start()
+            accumulate(n)
 
         for x in range(wide):
             ex, ey, ez = state[0, x], state[1, x], state[2, x]
@@ -235,103 +292,102 @@
         pulse = pulse_ref[n]
         ahead = n + 1
         side = lax.rem(ahead, 2)
-        corner_s[side, 0, 0:1, :] = (
-            state[0, last, 0:1, :]
-            + fac_v[last, 0:1, :] * (state[5, last, 0:1, :] - prev_row(state[5, last, 0:1, :]) - state[4, last, 0:1, :])
-            + src_v[last, 0:1, :] * pulse
-        )
-        corner_s[side, 0, 1:2, :] = fac_v[last, 0:1, :]
-        corner_s[side, 1, 0:1, :] = state[2, 0, 7:8, :] + fac_v[0, 7:8, :] * (
-            state[4, 0, 7:8, :] - (state[3, 0, 7:8, :] - prev_row(state[3, 0, 7:8, :]))
-        )
-        corner_s[side, 1, 1:2, :] = fac_v[0, 7:8, :]
-        for place, has in ((0, has_a), (1, has_b)):
-            @pl.when(has & (ahead < STEPS))
-            def _():
-                corner(ahead, place).start()
-
-        for has, index, there in (
-            (has_hx, 0, in_xe), (has_lx, 3, in_xh), (has_hz, 1, in_ze), (has_lz, 4, in_zh), (has_hx, 2, in_xr),
-        ):
-            @pl.when(has)
-            def _():
-                copy(index, there.at[slot], to_lx, there.at[slot], index).wait_recv()
-        for has, item in (
-            (has_lx, out_lx), (has_lz, out_lz), (has_lx, out_rx), (has_hx, out_hx), (has_hz, out_hz)
-        ):
-            @pl.when(has)
-            def _():
-                item.wait_send()
+        if more:
+            corner_s[side, 0, 0:1, :] = (
+                state[0, last, 0:1, :] + src_v[last, 0:1, :] * pulse + fac_v[last, 0:1, :]
+                * (state[5, last, 0:1, :] - prev_row(state[5, last, 0:1, :]) - state[4, last, 0:1, :])
+            )
+            corner_s[side, 0, 1:2, :] = fac_v[last, 0:1, :]
+            corner_s[side, 1, 0:1, :] = state[2, 0, 7:8, :] + fac_v[0, 7:8, :] * (
+                state[4, 0, 7:8, :] - (state[3, 0, 7:8, :] - prev_row(state[3, 0, 7:8, :]))
+            )
+            corner_s[side, 1, 1:2, :] = fac_v[0, 7:8, :]
+            begin(has_a, corner(ahead, 0))
+            begin(has_b, corner(ahead, 1))
+
+        for item, has_to, _ in now.values():
+            pl.when(has_to)(item.wait_send)
         for place, has_to, has_from in ((0, has_a, has_b), (1, has_b, has_a)):
-            @pl.when(has_from)
-            def _():
-                corner(n, place).wait_recv()
-
-            @pl.when(has_to)
-            def _():
-                corner(n, place).wait_send()
+            pl.when(has_to)(corner(n, place).wait_send)
+            pl.when(has_from)(corner(n, place).wait_recv)
+        receive(now, "xh", "ze0", "zh0")
         here = lax.rem(n, 4)
         corner_ex = in_c[here, 0, 0:1, :] + in_c[here, 0, 1:2, :] * mix[0:1, :]
         corner_ez = in_c[here, 1, 0:1, :] + in_c[here, 1, 1:2, :] * mix[1:2, :]
 
         ex, ey, ez = state[0, 0], state[1, 0], state[2, 0]
-        corner_x = jnp.where(top_row, wide_row(corner_ex), 0.0)
-        before_y = keep_lx * (in_xh[slot, 0] + s * ez - s * corner_x)
-        before_z = keep_lx * (in_xh[slot, 1] - s * ey)
-        face = in_ze[slot, 1, 0:1, :]
-        mix[0:1, :] = before_y[7:8, :] - s * (face - prev_row(face)) - s * in_ze[slot, 0, wide : wide + 1, :]
+        corner_x = jnp.where(top_row, wide_row(keep_hz * corner_ex), 0.0)
+        before_y = keep_lx * (in_all[slot, 2] + s * ez - s * corner_x)
+        before_z = keep_lx * (in_all[slot, 3] - s * ey)
+        face = in_all[slot, 4, half : half + 1, :]
+        mix[0:1, :] = before_y[7:8, :] - s * (face - prev_row(face)) - s * in_all[slot, 4, 2 * half : 2 * half + 1, :]
         for x in range(wide):
+            part, place = x // half, x % half
+            if x == half:
+                receive(now, "ze1", "zh1")
+            if x == last:
+                receive(now, "xe", "xr")
             ex, ey, ez = state[0, x], state[1, x], state[2, x]
-            above_x = wide_row(in_ze[slot, 0, x : x + 1, :])
-            above_y = wide_row(in_ze[slot, 1, x : x + 1, :])
-            hx = state[3, x] + jnp.where(top_row, s * above_y, 0.0)
-            hy = state[4, x] - jnp.where(top_row, s * above_x, 0.0)
+            above_x = wide_row(in_all[slot, 4 + part, place : place + 1, :])
+            above_y = wide_row(in_all[slot, 4 + part, half + place : half + place + 1, :])
+            hx = state[3, x] + jnp.where(top_row, (s * keep_hz) * above_y, 0.0)
+            hy = state[4, x] - jnp.where(top_row, (s * keep_hz) * above_x, 0.0)
             hz = state[5, x]
-            below_x = wide_row(in_zh[slot, 0, x : x + 1, :]) + s * ey
-            below_y = wide_row(in_zh[slot, 1, x : x + 1, :]) - s * ex
+            below_x = wide_row(in_all[slot, 6 + part, place : place + 1, :]) + s * ey
+            below_y = wide_row(in_all[slot, 6 + part, half + place : half + place + 1, :]) - s * ex
             if x == last:
-                hy = hy + s * in_xe[slot, 1]
-                hz = hz - s * in_xe[slot, 0]
-                below_y = below_y + s * wide_row(corner_ez)
-                face = in_xe[slot, 0, 0:1, :]
-                mix[1:2, :] = -below_y[0:1, :] - s * in_xr[slot] - s * (face - prev_row(face))
+                hy = hy + (s * keep_hx) * in_all[slot, 1]
+                hz = hz - (s * keep_hx) * in_all[slot, 0]
+                below_y = below_y + s * wide_row(keep_hx * corner_ez)
+                face = in_all[slot, 0, 0:1, :]
+                mix[1:2, :] = -below_y[0:1, :] - s * in_all[slot, 8, 0:1, :] - s * (face - prev_row(face))
             down_x = jnp.where(first_row, keep_lz * below_x, pltpu.roll(hx, 1, 0))
             down_y = jnp.where(first_row, keep_lz * below_y, pltpu.roll(hy, 1, 0))
             fac = fac_v[x]
-            state[0, x] = ex + fac * ((hz - prev_y(hz)) - (hy - down_y)) + src_v[x] * pulse
-            state[1, x] = ey + fac * ((hx - down_x) - (hz - before_z))
-            state[2, x] = ez + fac * ((hy - before_y) - (hx - prev_y(hx)))
+            ex = ex + fac * ((hz - prev_y(hz)) - (hy - down_y)) + src_v[x] * pulse
+            ey = ey + fac * ((hx - down_x) - (hz - before_z))
+            ez = ez + fac * ((hy - before_y) - (hx - prev_y(hx)))
+            keep_rows(x, ex, ey, ez)
+            state[0, x] = ex
+            state[1, x] = ey
+            state[2, x] = ez
             state[3, x] = hx
             state[4, x] = hy
             state[5, x] = hz
             before_y, before_z = hy, hz
-
-        @pl.when(at_exit)
-        def _():
-            for x in range(wide):
-                rows_top[0, x : x + 1, :] = state[0, x, 7:8, :]
-                rows_top[1, x : x + 1, :] = state[1, x, 7:8, :]
-            for f in range(2):
-                for part in range(2):
-                    weight = turn_ref[4 * n + 2 * f + part]
-                    for c in range(2):
-                        spec[4 * f + 2 * c + part] += weight * rows_top[c]
-
+            if more:
+                if x == 0:
+                    send(later, "xe", "xr")
+                if x == half - 1:
+                    send(later, "ze0")
+                if x == last:
+                    send(later, "ze1")
+                if x > 0:
+                    advance_h(x - 1)
+                if x == half:
+                    send(later, "zh0")
+        if more:
+            advance_h(last)
+            send(later, "zh1", "xh")
+
+    def full_step(n, carry):
+        one_step(n, True)
         return carry
 
-    lax.fori_loop(0, STEPS, one_step, 0)
+    lax.fori_loop(0, STEPS - 1, full_step, 0)
+    one_step(STEPS - 1, False)
 
     lane_group = lax.broadcasted_iota(jnp.int32, (8, 128), 1) // 8
-    half = planes.shape[1] // 2
+    middle = planes.shape[1] // 2
 
     def place_plane(index, value, lanes):
         f, c, part = index // 4, index // 2 % 2, index % 2
         base = 32 * f + 16 * c
         if part == 0:
             planes[base : base + 8, pl.ds(lanes, value.shape[1])] = value
-            planes[base + 8 : base + 16, pl.ds(half + lanes, value.shape[1])] = value
+            planes[base + 8 : base + 16, pl.ds(middle + lanes, value.shape[1])] = value
         else:
-            planes[base : base + 8, pl.ds(half + lanes, value.shape[1])] = -value
+            planes[base : base + 8, pl.ds(middle + lanes, value.shape[1])] = -value
             planes[base + 8 : base + 16, pl.ds(lanes, value.shape[1])] = value
 
     def transform(high, low, result):
@@ -357,19 +413,19 @@
     def _():
         for item in tables:
             item.wait()
+        accumulate(STEPS)
         for index in range(8):
             place_plane(index, spec[index], 0)
         transform(col_high, col_low, out_a)
 
-        def send_a(i, carry):
-            peer = lax.rem(pos_x + i, count_x)
-            pltpu.make_async_remote_copy(
+        def send_a(peer, may_be_own):
+            item = pltpu.make_async_remote_copy(
                 src_ref=tile(out_a, peer), dst_ref=in_a.at[pos_x], send_sem=tail_send.at[0],
                 recv_sem=tail_recv.at[0], device_id=(exit_z, peer), device_id_type=MESH,
-            ).start()
-            return carry
-
-        lax.fori_loop(1, count_x, send_a, 0)
+            )
+            begin(peer != pos_x, item) if may_be_own else item.start()
+
+        for_peers(send_a)
         in_a[pos_x] = out_a[pl.ds(pl.multiple_of(8 * pos_x, 8), 8), :]
         others = in_a.at[pl.ds(0, count_x - 1)]
         whole = pltpu.make_async_remote_copy(
@@ -389,19 +445,14 @@
         transform(row_high, row_low, out_b)
         mine = lax.rem(pos_x, group)
 
-        def send_b(i, carry):
-            peer = lax.rem(pos_x + i, count_x)
-            pltpu.make_async_remote_copy(
+        def send_b(peer, may_be_own):
+            item = pltpu.make_async_remote_copy(
                 src_ref=tile(out_b, peer), dst_ref=in_b.at[mine], send_sem=tail_send.at[1],
                 recv_sem=tail_recv.at[1], device_id=(target_z, peer), device_id_type=MESH,
-            ).start()
-            return carry
-
-        lax.fori_loop(1, count_x, send_b, 0)
-
-        @pl.when(target_z != exit_z)
-        def _():
-            send_b(0, 0)
+            )
+            begin((target_z != exit_z) | (peer != pos_x), item) if may_be_own else item.start()
+
+        for_peers(send_b)
 
         @pl.when(target_z == exit_z)
         def _():
@@ -476,25 +527,21 @@
             pltpu.SMEM(eps_table.shape, f32),
             pltpu.SMEM(kerr_table.shape, f32),
             pltpu.SMEM((STEPS,), f32),
-            pltpu.SMEM((4 * STEPS,), f32),
+            pltpu.SMEM((4 * STEPS + 4,), f32),
             pltpu.SemaphoreType.DMA((5,)),
             pltpu.VMEM((wide, deep, span), f32),
             pltpu.VMEM((wide, deep, span), f32),
             pltpu.VMEM((wide, deep, span), f32),
             pltpu.VMEM((wide, deep, span), f32),
-            pltpu.VMEM((2, wide + 1, span), f32),
-            pltpu.VMEM((2, wide, span), f32),
+            pltpu.VMEM((2, 8, span), f32),
+            pltpu.VMEM((2, 8, span), f32),
             pltpu.VMEM((2, 8, span), f32),
             pltpu.VMEM((2, 2, 2, span), f32),
             pltpu.VMEM((2, span), f32),
-            pltpu.VMEM((2, 2, deep, span), f32),
-            pltpu.VMEM((2, 1, span), f32),
-            pltpu.VMEM((2, 2, deep, span), f32),
-            pltpu.VMEM((2, 2, wide + 1, span), f32),
-            pltpu.VMEM((2, 2, wide, span), f32),
+            pltpu.VMEM((2, 9, 8, span), f32),
             pltpu.VMEM((4, 2, 2, span), f32),
-            pltpu.SemaphoreType.DMA((5,)),
-            pltpu.SemaphoreType.DMA((2, 5)),
+            pltpu.SemaphoreType.DMA((7,)),
+            pltpu.SemaphoreType.DMA((2, 7)),
             pltpu.SemaphoreType.DMA((2, 2)),
             pltpu.SemaphoreType.DMA((4, 2)),
         ],

time: 135 us -> 130 us (0.963)
  Pallas kernels: 131 us -> 125 us
    pallas_call x1, Pallas kernels: 131 us -> 125 us  [march(): pl.pallas_call(functools.partial(step_kernel, count_z, count_x), out_shap...]
where the time goes in v4:
time: 130 us; the launch traced here: 129 us
  Pallas kernels  125 us (96%)
  local copies, waits for them, and re-layouts  3.28 us (3%)
    pallas_call x1, Pallas kernels, march(): pl.pallas_call(functools.partial(step_kernel, count_z, count_x), out_shap...  125 us
    unnamed x2, local copies, waits for them, and re-layouts  3.28 us

profile of v4, /device:TPU:1, one launch (start us, length us, event | category | flops | bytes accessed | tf_op | source)
XLA Modules:
  0.0 129.4 jit_solution(2457183389672505245)
XLA Ops:
  0.6 125.5 %march.1 = (f32[6,6,8,512]{3,2,1,0:T(8,128)}, f32[6,8,64]{2,1,0:T(8,128)}) custom-call(f32[6,6,8,512]{3,2,1,0:T(8,128)} %fields_hbm.1, s32[6,8,512]{2,1,0:T(8,128)} %material_hbm.1, s32[6,8,512]{2,1,0:T(8,128)} %mask_hbm.1, f32[4]{0:T(128)} %eps_hbm.1, f32[4]{0:T(128)} %kerr_hbm.1, bf16[2,512,1024]{2,1,0:T(8,128)(2,1)} %constant.8.clone.col_high_hbm, ...), custom_call_target="tpu_custom_call" | custom-call | tf_op jit(solution)/shard_map/march/pallas_call | solution.py:506
  126.1 1.9 %copy.13 = f32[6,6,8,512]{3,2,1,0:T(8,128)} copy(f32[6,6,8,512]{3,2,1,0:T(8,128)} %get-tuple-element.4) | data formatting | bytes 1179648
  128.1 1.3 %copy.14 = f32[6,8,64]{2,1,0:T(8,128)} copy(f32[6,8,64]{2,1,0:T(8,128)} %get-tuple-element.5) | data formatting | bytes 24576

commit v5 on v4

--- a/solution.py
+++ b/solution.py
@@ -50,8 +50,8 @@
 def step_kernel(
     count_z, count_x,
     fields_hbm, material_hbm, mask_hbm, eps_hbm, kerr_hbm, col_high_hbm, col_low_hbm, row_high_hbm, row_low_hbm,
-    state, image,
-    spec, col_high, col_low, row_high, row_low, table_sem, planes, out_a, in_a, out_b, in_b, tail_send, tail_recv,
+    fields_out, image,
+    state, spec, col_high, col_low, row_high, row_low, table_sem, planes, out_a, in_a, out_b, in_b, tail_send, tail_recv,
     material_ref, mask_ref, eps_ref, kerr_ref, pulse_ref, turn_ref, load_sem,
     eps_v, kerr_v, src_v, fac_v,
     rows_e, rows_h, rows_top, corner_s, mix,
@@ -109,11 +109,6 @@
         lax.fori_loop(0, runs, run, 0)
 
     barrier = pltpu.get_barrier_semaphore()
-    for has, target in neighbours:
-        @pl.when(has)
-        def _():
-            pl.semaphore_signal(barrier, inc=1, device_id=target, device_id_type=MESH)
-
     exit_z = count_z - 1
     at_exit = pos_z == exit_z
     group = count_x // count_z
@@ -139,6 +134,14 @@
             pl.when(peer != pos_x)(signal) if may_be_own else signal()
 
         for_peers(greet)
+
+    for has, target in neighbours:
+        @pl.when(has)
+        def _():
+            pl.semaphore_signal(barrier, inc=1, device_id=target, device_id_type=MESH)
+
+    @pl.when(at_exit)
+    def _():
         for item in tables:
             item.start()
 
@@ -307,38 +310,24 @@
 
         for item, has_to, _ in now.values():
             pl.when(has_to)(item.wait_send)
-        for place, has_to, has_from in ((0, has_a, has_b), (1, has_b, has_a)):
-            pl.when(has_to)(corner(n, place).wait_send)
-            pl.when(has_from)(corner(n, place).wait_recv)
-        receive(now, "xh", "ze0", "zh0")
-        here = lax.rem(n, 4)
-        corner_ex = in_c[here, 0, 0:1, :] + in_c[here, 0, 1:2, :] * mix[0:1, :]
-        corner_ez = in_c[here, 1, 0:1, :] + in_c[here, 1, 1:2, :] * mix[1:2, :]
-
-        ex, ey, ez = state[0, 0], state[1, 0], state[2, 0]
-        corner_x = jnp.where(top_row, wide_row(keep_hz * corner_ex), 0.0)
-        before_y = keep_lx * (in_all[slot, 2] + s * ez - s * corner_x)
-        before_z = keep_lx * (in_all[slot, 3] - s * ey)
-        face = in_all[slot, 4, half : half + 1, :]
-        mix[0:1, :] = before_y[7:8, :] - s * (face - prev_row(face)) - s * in_all[slot, 4, 2 * half : 2 * half + 1, :]
-        for x in range(wide):
+        def complete_z(x):
             part, place = x // half, x % half
-            if x == half:
-                receive(now, "ze1", "zh1")
-            if x == last:
-                receive(now, "xe", "xr")
-            ex, ey, ez = state[0, x], state[1, x], state[2, x]
             above_x = wide_row(in_all[slot, 4 + part, place : place + 1, :])
             above_y = wide_row(in_all[slot, 4 + part, half + place : half + place + 1, :])
             hx = state[3, x] + jnp.where(top_row, (s * keep_hz) * above_y, 0.0)
             hy = state[4, x] - jnp.where(top_row, (s * keep_hz) * above_x, 0.0)
-            hz = state[5, x]
+            return hx, hy, state[5, x]
+
+        def advance_e(x, magnetic, before_y, before_z, corner_row):
+            part, place = x // half, x % half
+            hx, hy, hz = magnetic
+            ex, ey, ez = state[0, x], state[1, x], state[2, x]
             below_x = wide_row(in_all[slot, 6 + part, place : place + 1, :]) + s * ey
             below_y = wide_row(in_all[slot, 6 + part, half + place : half + place + 1, :]) - s * ex
             if x == last:
                 hy = hy + (s * keep_hx) * in_all[slot, 1]
                 hz = hz - (s * keep_hx) * in_all[slot, 0]
-                below_y = below_y + s * wide_row(keep_hx * corner_ez)
+                below_y = below_y + s * wide_row(keep_hx * corner_row)
                 face = in_all[slot, 0, 0:1, :]
                 mix[1:2, :] = -below_y[0:1, :] - s * in_all[slot, 8, 0:1, :] - s * (face - prev_row(face))
             down_x = jnp.where(first_row, keep_lz * below_x, pltpu.roll(hx, 1, 0))
@@ -354,21 +343,48 @@
             state[3, x] = hx
             state[4, x] = hy
             state[5, x] = hz
-            before_y, before_z = hy, hz
-            if more:
-                if x == 0:
-                    send(later, "xe", "xr")
-                if x == half - 1:
-                    send(later, "ze0")
-                if x == last:
-                    send(later, "ze1")
-                if x > 0:
-                    advance_h(x - 1)
-                if x == half:
-                    send(later, "zh0")
+
+        receive(now, "ze0", "zh0")
+        first_h = complete_z(0)
+        before = first_h
+        for x in range(1, last):
+            if x == half:
+                receive(now, "ze1", "zh1")
+            magnetic = complete_z(x)
+            advance_e(x, magnetic, before[1], before[2], None)
+            before = magnetic
+            if more and x > 1:
+                advance_h(x - 1)
+
+        for place, has_to, has_from in ((0, has_a, has_b), (1, has_b, has_a)):
+            pl.when(has_to)(corner(n, place).wait_send)
+            pl.when(has_from)(corner(n, place).wait_recv)
+        here = lax.rem(n, 4)
+        corner_ex = in_c[here, 0, 0:1, :] + in_c[here, 0, 1:2, :] * mix[0:1, :]
+        corner_ez = in_c[here, 1, 0:1, :] + in_c[here, 1, 1:2, :] * mix[1:2, :]
+        receive(now, "xe", "xr")
+        advance_e(last, complete_z(last), before[1], before[2], corner_ez)
         if more:
             advance_h(last)
-            send(later, "zh1", "xh")
+            send(later, "xh")
+        receive(now, "xh")
+        ex, ey, ez = state[0, 0], state[1, 0], state[2, 0]
+        corner_x = jnp.where(top_row, wide_row(keep_hz * corner_ex), 0.0)
+        before_y = keep_lx * (in_all[slot, 2] + s * ez - s * corner_x)
+        before_z = keep_lx * (in_all[slot, 3] - s * ey)
+        face = in_all[slot, 4, half : half + 1, :]
+        mix[0:1, :] = (
+            before_y[7:8, :] - s * (face - prev_row(face)) - s * in_all[slot, 4, 2 * half : 2 * half + 1, :]
+        )
+        advance_e(0, first_h, before_y, before_z, None)
+        if more:
+            send(later, "xe", "xr", "ze0")
+        if more:
+            send(later, "ze1")
+            advance_h(0)
+            send(later, "zh0")
+            advance_h(last - 1)
+            send(later, "zh1")
 
     def full_step(n, carry):
         one_step(n, True)
@@ -376,6 +392,8 @@
 
     lax.fori_loop(0, STEPS - 1, full_step, 0)
     one_step(STEPS - 1, False)
+    leave = pltpu.make_async_copy(state, fields_out, load_sem.at[0])
+    leave.start()
 
     lane_group = lax.broadcasted_iota(jnp.int32, (8, 128), 1) // 8
     middle = planes.shape[1] // 2
@@ -489,6 +507,8 @@
             recv_sem=tail_recv.at[1], device_id=(exit_z, pos_x), device_id_type=MESH,
         )
 
+    leave.wait()
+
     @pl.when(own)
     def _():
         sent(count_x - 1).wait_send()
@@ -510,8 +530,9 @@
             jax.ShapeDtypeStruct((wide, 8, span // count_z), f32),
         ),
         in_specs=[pl.BlockSpec(memory_space=pl.ANY)] * 9,
-        out_specs=(vmem, vmem),
+        out_specs=(pl.BlockSpec(memory_space=pl.ANY), vmem),
         scratch_shapes=[
+            pltpu.VMEM(fields.shape, f32),
             pltpu.VMEM((8, 8, span), f32),
             *(pltpu.VMEM(table.shape, jnp.bfloat16) for table in tables),
             pltpu.SemaphoreType.DMA((4,)),

time: 130 us -> 128 us (0.985)
  Pallas kernels: 125 us -> 123 us
    pallas_call x1, Pallas kernels: 125 us -> 123 us  [march(): pl.pallas_call(functools.partial(step_kernel, count_z, count_x), out_shap...]
where the time goes in v5:
time: 128 us; the launch traced here: 127 us
  Pallas kernels  123 us (96%)
  local copies, waits for them, and re-layouts  3.28 us (3%)
    pallas_call x1, Pallas kernels, march(): pl.pallas_call(functools.partial(step_kernel, count_z, count_x), out_shap...  123 us
    unnamed x2, local copies, waits for them, and re-layouts  3.28 us

profile of v5, /device:TPU:1, one launch (start us, length us, event | category | flops | bytes accessed | tf_op | source)
XLA Modules:
  0.0 127.4 jit_solution(8459272762242858171)
XLA Ops:
  0.6 123.5 %march.1 = (f32[6,6,8,512]{3,2,1,0:T(8,128)}, f32[6,8,64]{2,1,0:T(8,128)}) custom-call(f32[6,6,8,512]{3,2,1,0:T(8,128)} %fields_hbm.1, s32[6,8,512]{2,1,0:T(8,128)} %material_hbm.1, s32[6,8,512]{2,1,0:T(8,128)} %mask_hbm.1, f32[4]{0:T(128)} %eps_hbm.1, f32[4]{0:T(128)} %kerr_hbm.1, bf16[2,512,1024]{2,1,0:T(8,128)(2,1)} %constant.8.clone.col_high_hbm, ...), custom_call_target="tpu_custom_call" | custom-call | tf_op jit(solution)/shard_map/march/pallas_call | solution.py:526
  124.1 1.9 %copy.13 = f32[6,6,8,512]{3,2,1,0:T(8,128)} copy(f32[6,6,8,512]{3,2,1,0:T(8,128)} %get-tuple-element.4) | data formatting | bytes 1179648
  126.1 1.3 %copy.14 = f32[6,8,64]{2,1,0:T(8,128)} copy(f32[6,8,64]{2,1,0:T(8,128)} %get-tuple-element.5) | data formatting | bytes 24576

commit v6 on v5

--- a/solution.py
+++ b/solution.py
@@ -573,9 +573,49 @@
     )(fields, material, mask, eps_table, kerr_table, *(jnp.asarray(table) for table in tables))
 
 
+def hand_over_kernel(fields_ref, image_ref, fields_out, image_out, fields_v, image_v, into, out):
+    stages = [
+        (
+            pltpu.make_async_copy(fields_ref.at[i], fields_v.at[i], into.at[i]),
+            pltpu.make_async_copy(fields_v.at[i], fields_out.at[i], out.at[i]),
+        )
+        for i in range(6)
+    ]
+    stages.append((
+        pltpu.make_async_copy(image_ref, image_v, into.at[6]), pltpu.make_async_copy(image_v, image_out, out.at[6])
+    ))
+    for first, _ in stages:
+        first.start()
+    for first, second in stages:
+        first.wait()
+        second.start()
+    for _, second in stages:
+        second.wait()
+
+
+def hand_over(fields, image):
+    anywhere = pl.BlockSpec(memory_space=pl.ANY)
+    return pl.pallas_call(
+        hand_over_kernel,
+        out_shape=(
+            jax.ShapeDtypeStruct(fields.shape, jnp.float32), jax.ShapeDtypeStruct(image.shape, jnp.float32)
+        ),
+        in_specs=[anywhere] * 2,
+        out_specs=(anywhere,) * 2,
+        scratch_shapes=[
+            pltpu.VMEM(fields.shape, jnp.float32),
+            pltpu.VMEM(image.shape, jnp.float32),
+            pltpu.SemaphoreType.DMA((7,)),
+            pltpu.SemaphoreType.DMA((7,)),
+        ],
+        compiler_params=pltpu.CompilerParams(vmem_limit_bytes=60 * 1024 * 1024),
+        name="hand_over",
+    )(fields, image)
+
+
 def local(fields, material, source_mask, eps_table, kerr_table):
     count_x, count_z = lax.axis_size("lat"), lax.axis_size("depth")
-    return march(count_z, count_x, fields, material, source_mask, eps_table, kerr_table)
+    return hand_over(*march(count_z, count_x, fields, material, source_mask, eps_table, kerr_table))
 
 
 def solution(mesh):

time: 128 us -> 127 us (level)
  local copies, waits for them, and re-layouts: 3.28 us -> 0 us
  Pallas kernels: 123 us -> 125 us
    unnamed x2 -> x0, local copies, waits for them, and re-layouts: 3.28 us -> none
    pallas_call x0 -> x1, Pallas kernels: none -> 1.89 us  [hand_over(): pl.pallas_call(hand_over_kernel, out_shape=(jax.ShapeDtypeStruct(fields.s...]
where the time goes in v6:
time: 127 us; the launch traced here: 126 us
  Pallas kernels  125 us (98%)
    pallas_call x1, Pallas kernels, march(): pl.pallas_call(functools.partial(step_kernel, count_z, count_x), out_shap...  124 us

profile of v6, /device:TPU:1, one launch (start us, length us, event | category | flops | bytes accessed | tf_op | source)
XLA Modules:
  0.0 126.0 jit_solution(6292286647561672119)
XLA Ops:
  0.6 123.5 %march.1 = (f32[6,6,8,512]{3,2,1,0:T(8,128)}, f32[6,8,64]{2,1,0:T(8,128)}) custom-call(f32[6,6,8,512]{3,2,1,0:T(8,128)} %fields_hbm.1, s32[6,8,512]{2,1,0:T(8,128)} %material_hbm.1, s32[6,8,512]{2,1,0:T(8,128)} %mask_hbm.1, f32[4]{0:T(128)} %eps_hbm.1, f32[4]{0:T(128)} %kerr_hbm.1, bf16[2,512,1024]{2,1,0:T(8,128)(2,1)} %constant.8.clone.col_high_hbm, ...), custom_call_target="tpu_custom_call" | custom-call | tf_op jit(solution)/shard_map/march/pallas_call | solution.py:526
  124.1 1.9 %hand_over.1 = (f32[6,6,8,512]{3,2,1,0:T(8,128)}, f32[6,8,64]{2,1,0:T(8,128)}) custom-call(f32[6,6,8,512]{3,2,1,0:T(8,128)} %get-tuple-element.4.fields_ref, f32[6,8,64]{2,1,0:T(8,128)} %get-tuple-element.5.image_ref), custom_call_target="tpu_custom_call" | custom-call | tf_op jit(solution)/shard_map/hand_over/pallas_call | solution.py:598
